TPU v7x, 128 devices: a whole 4x4x4 slice. The times are simulated.
128 devices in a mesh: ctx: 8 (over y, core), tp: 16 (over x, z).
Axes of the slice: x: 4, y: 4, z: 4, core: 2. Of those that a mesh axis runs over, the one named last changes fastest.
Arguments:
- tokens: bfloat16 [16384, 2048], P('ctx', 'tp'), may hold values from -6 to 6
- cotangent: bfloat16 [16384, 2048], P('ctx', 'tp'), may hold values from -6 to 6
- w_query: bfloat16 [2048, 2048], P(None, 'tp'), may hold values from -0.243067956 to 0.243067956
- w_key: bfloat16 [2048, 2048], P(None, 'tp'), may hold values from -0.243067956 to 0.243067956
- w_value: bfloat16 [2048, 2048], P(None, 'tp'), may hold values from -0.125 to 0.125
- w_out: bfloat16 [2048, 2048], P('tp'), may hold values from -0.125 to 0.125
Outputs:
- token_grad: bfloat16 [16384, 2048], P('ctx', 'tp')
- query_grad: float32 [2048, 2048], P(None, 'tp')
- key_grad: float32 [2048, 2048], P(None, 'tp')
- value_grad: float32 [2048, 2048], P(None, 'tp')
- out_grad: float32 [2048, 2048], P('tp')
All inputs are finite; a program needn't handle non-finite values.
Results may differ from a plain program's by a relative error of at most 0.017.
The roundings to bfloat16 on the way count: a program that leaves them out, or rounds other values in their place, can miss the bound.
Values may be sent and summed in bfloat16 or wider, within the bound.
No kernel may reach another device: no remote copies, remote signals or barrier semaphores. Data moves between devices by JAX's collectives and lax.ppermute only.
A program may use at most 192 MiB of HBM per device.

v0:
```python
import math

import jax
import jax.numpy as jnp
from jax import lax
from jax.sharding import PartitionSpec as P

DH = 128
RATIO = 16


def from_partner(value, axis, bit):
    mask = 2**bit
    pairs = [(source, source ^ mask) for source in range(lax.axis_size(axis))]
    return lax.ppermute(value, axis, pairs)


def pool_rows(values, width):
    return jnp.mean(
        values.reshape(values.shape[0] // width, width, values.shape[1]), axis=1, dtype=jnp.float32
    )


def contract_rows(left, right):
    return lax.dot_general(
        left, right, (((0,), (0,)), ((), ())), preferred_element_type=jnp.float32
    )


def contract_cols(left, right):
    return lax.dot_general(
        left, right, (((1,), (1,)), ((), ())), preferred_element_type=jnp.float32
    )


def split_rows(packed, row_counts):
    pieces = []
    offset = 0
    for number in row_counts:
        pieces.append(packed[:, offset : offset + number])
        offset = offset + number
    return pieces


def spread_rows(grads, width):
    return jnp.broadcast_to(
        grads[:, None, :] / width, (grads.shape[0], width, grads.shape[1])
    ).reshape(grads.shape[0] * width, grads.shape[1])


def body(tokens, cotangent, w_query, w_key, w_value, w_out):
    feats = lax.all_gather(tokens, "tp", axis=1, tiled=True)
    tok_rows = feats.shape[0]
    head_cols = w_query.shape[1]
    heads = head_cols // DH
    levels = lax.axis_size("ctx").bit_length() - 1
    coarse = tok_rows // RATIO
    score_scale = DH ** (-0.5)
    ctx_index = lax.axis_index("ctx")
    queries = jnp.dot(feats, w_query, preferred_element_type=jnp.float32).astype(jnp.bfloat16)
    key_rows = jnp.dot(feats, w_key, preferred_element_type=jnp.float32).astype(jnp.bfloat16)
    value_rows = jnp.dot(feats, w_value, preferred_element_type=jnp.float32).astype(jnp.bfloat16)
    own_pooled = []
    for l in range(levels):
        width = RATIO * 2**l
        own_pooled.append(
            jnp.stack([pool_rows(key_rows, width), pool_rows(value_rows, width)]).astype(
                jnp.bfloat16
            )
        )
    partners = []
    grouped = list(own_pooled)
    for m in range(levels):
        packed = jnp.concatenate(grouped[m:], axis=1)
        received = from_partner(packed, "ctx", m)
        pieces = split_rows(received, [g.shape[1] for g in grouped[m:]])
        partners.append(pieces[0])
        is_lower = ctx_index >> m & 1 == 0
        for j in range(m + 1, levels):
            mine = grouped[j]
            theirs = pieces[j - m]
            grouped[j] = jnp.where(
                is_lower,
                jnp.concatenate([mine, theirs], axis=1),
                jnp.concatenate([theirs, mine], axis=1),
            )
    keys_all = jnp.concatenate([key_rows] + [p[0] for p in partners], axis=0)
    values_all = jnp.concatenate([value_rows] + [p[1] for p in partners], axis=0)
    bias_all = jnp.concatenate(
        [jnp.zeros((tok_rows,), jnp.float32)]
        + [jnp.full((coarse,), math.log(RATIO * 2**l), jnp.float32) for l in range(levels)]
    )
    query_heads = queries.reshape(tok_rows, heads, DH)
    key_heads = keys_all.reshape(-1, heads, DH)
    value_heads = values_all.reshape(-1, heads, DH)
    scores = (
        jnp.einsum("thd,khd->htk", query_heads, key_heads, preferred_element_type=jnp.float32)
        * score_scale
        + bias_all[None, None, :]
    )
    peak = jnp.max(scores, axis=-1, keepdims=True)
    expo = jnp.exp(scores - peak)
    probs = expo / jnp.sum(expo, axis=-1, keepdims=True)
    probs_low = probs.astype(jnp.bfloat16)
    attended = (
        jnp.einsum("htk,khd->thd", probs_low, value_heads, preferred_element_type=jnp.float32)
        .reshape(tok_rows, head_cols)
        .astype(jnp.bfloat16)
    )
    dy_full = lax.all_gather(cotangent, "tp", axis=1, tiled=True)
    d_attended = contract_cols(dy_full, w_out).astype(jnp.bfloat16)
    d_att_heads = d_attended.reshape(tok_rows, heads, DH)
    d_probs = jnp.einsum(
        "thd,khd->htk", d_att_heads, value_heads, preferred_element_type=jnp.float32
    )
    delta = jnp.sum(probs * d_probs, axis=-1, keepdims=True)
    d_scores = (score_scale * probs * (d_probs - delta)).astype(jnp.bfloat16)
    d_queries = (
        jnp.einsum("htk,khd->thd", d_scores, key_heads, preferred_element_type=jnp.float32)
        .reshape(tok_rows, head_cols)
        .astype(jnp.bfloat16)
    )
    d_keys_all = jnp.einsum(
        "htk,thd->khd", d_scores, query_heads, preferred_element_type=jnp.float32
    ).reshape(-1, head_cols)
    d_values_all = jnp.einsum(
        "htk,thd->khd", probs_low, d_att_heads, preferred_element_type=jnp.float32
    ).reshape(-1, head_cols)
    d_partners = []
    for m in range(levels):
        low = tok_rows + m * coarse
        d_partners.append(
            jnp.stack([d_keys_all[low : low + coarse], d_values_all[low : low + coarse]])
        )
    own_grads = [None] * levels
    for m in reversed(range(levels)):
        is_lower = ctx_index >> m & 1 == 0
        sends = [d_partners[m]]
        keeps = []
        row_counts = [coarse]
        for j in range(m + 1, levels):
            half_rows = coarse >> j << m
            merged = own_grads[j]
            first_half = merged[:, :half_rows]
            second_half = merged[:, half_rows:]
            keeps.append(jnp.where(is_lower, first_half, second_half))
            sends.append(jnp.where(is_lower, second_half, first_half))
            row_counts.append(half_rows)
        received = from_partner(jnp.concatenate(sends, axis=1), "ctx", m)
        pieces = split_rows(received, row_counts)
        own_grads[m] = pieces[0]
        for j in range(m + 1, levels):
            own_grads[j] = keeps[j - m - 1] + pieces[j - m]
    key_total = d_keys_all[:tok_rows]
    value_total = d_values_all[:tok_rows]
    for l in range(levels):
        width = RATIO * 2**l
        key_total = key_total + spread_rows(own_grads[l][0], width)
        value_total = value_total + spread_rows(own_grads[l][1], width)
    d_keys = key_total.astype(jnp.bfloat16)
    d_values = value_total.astype(jnp.bfloat16)
    query_grad, key_grad, value_grad, out_grad = lax.psum(
        (
            contract_rows(feats, d_queries),
            contract_rows(feats, d_keys),
            contract_rows(feats, d_values),
            contract_rows(attended, dy_full),
        ),
        "ctx",
    )
    partial_grad = (
        contract_cols(d_queries, w_query)
        + contract_cols(d_keys, w_key)
        + contract_cols(d_values, w_value)
    )
    token_grad = lax.psum_scatter(partial_grad, "tp", scatter_dimension=1, tiled=True).astype(
        jnp.bfloat16
    )
    return (token_grad, query_grad, key_grad, value_grad, out_grad)


def solution(mesh):
    return jax.shard_map(
        body,
        mesh=mesh,
        in_specs=(
            P("ctx", "tp"),
            P("ctx", "tp"),
            P(None, "tp"),
            P(None, "tp"),
            P(None, "tp"),
            P("tp", None),
        ),
        out_specs=(P("ctx", "tp"), P(None, "tp"), P(None, "tp"), P(None, "tp"), P("tp", None)),
        check_vma=False,
    )
```

profile of v0, /device:TPU:1, one launch (start us, length us, event | category | flops | bytes accessed | tf_op | source)
XLA Modules:
  0.0 499.2 jit_solution(17159034873049198242)
XLA Ops:
  8.7 82.3 %all-gather.3.cloned.1.call-done = bf16[2048,2048]{1,0:T(8,128)(2,1)} async-done(((bf16[2048,128]{1,0:T(8,128)(2,1)}), bf16[2048,2048]{1,0:T(8,128)(2,1)}) %all-gather.3.cloned.1.call-update) | async-done | bytes 8388624 | tf_op jit(solution)/shard_map/all_gather | solution.py:52
  91.0 5.9 %bitcast_reduce_fusion = (f32[32,128]{1,0:T(8,128)S(1)}, bf16[2048,128]{1,0:T(8,128)(2,1)S(1)}) fusion(bf16[2048,2048]{1,0:T(8,128)(2,1)} %all-gather.3.cloned.1.call-done, bf16[2048,128]{1,0:T(8,128)(2,1)} %param.10), kind=kOutput, calls=%fused_computation.35 | convolution fusion | flops 1074524160 | bytes 9453568 | tf_op jit(solution)/shard_map/dot_general | solution.py:62
  104.3 66.6 %all-gather.5.cloned.1.call-done = bf16[2048,2048]{1,0:T(8,128)(2,1)} async-done(((bf16[2048,128]{1,0:T(8,128)(2,1)}), bf16[2048,2048]{1,0:T(8,128)(2,1)}) %all-gather.5.cloned.1.call-update) | async-done | bytes 8388624 | tf_op jit(solution)/shard_map/all_gather | solution.py:110
  170.9 5.8 %convolution_convert_fusion = bf16[2048,128]{1,0:T(8,128)(2,1)S(1)} fusion(bf16[2048,2048]{1,0:T(8,128)(2,1)} %all-gather.5.cloned.1.call-done, bf16[128,2048]{1,0:T(8,128)(2,1)} %param.11), kind=kOutput, calls=%fused_computation.17 | convolution fusion | flops 1074003968 | bytes 9437184 | tf_op jit(solution)/shard_map/dot_general | solution.py:31
  180.4 3.3 collective-permute-start.2
  185.6 8.3 %fusion = (f32[2048]{0:T(1024)S(1)}, f32[2048,2432]{1,0:T(8,128)}) fusion(f32[2432]{0:T(1024)S(1)} %copy-done.9, bf16[2048,128]{1,0:T(8,128)(2,1)S(1)} %convolution_convert_fusion.1, bf16[128,128]{1,0:T(8,128)(2,1)S(1)} %get-tuple-element.32, bf16[128,128]{1,0:T(8,128)(2,1)S(1)} %get-tuple-element.28, bf16[128,128]{1,0:T(8,128)(2,1)S(1)} %get-tuple-element.26, ...), kind=kOutput, calls=%fused_computation.4 | convolution fusion | flops 1292498944 | bytes 21087744 | tf_op jit(solution)/shard_map/thd,khd->htk/dot_general | solution.py:97
  193.9 10.7 %fusion.2 = f32[2048]{0:T(1024)S(1)} fusion(f32[2048,2432]{1,0:T(8,128)} %get-tuple-element.41, f32[2048]{0:T(1024)S(1)} %get-tuple-element.40, f32[2432]{0:T(1024)S(1)} %copy-done.9), kind=kLoop, calls=%fused_computation.7 | loop fusion | flops 19920896 | bytes 19949056 | tf_op jit(solution)/shard_map/reduce_sum | solution.py:103
  204.5 20.6 %multiply_reduce_fusion = (f32[2048]{0:T(1024)S(1)}, f32[2048,2432]{1,0:T(8,128)}, f32[2048,2432]{1,0:T(8,128)}) fusion(f32[2048]{0:T(1024)S(1)} %fusion.2, f32[2048]{0:T(1024)S(1)} %get-tuple-element.40, f32[2432]{0:T(1024)S(1)} %copy-done.9, f32[2048,2432]{1,0:T(8,128)} %get-tuple-element.41, bf16[2048,128]{1,0:T(8,128)(2,1)S(1)} %convolution_convert_fusion, ...), kind=kOutput, calls=%fused_computation.1 | convolution fusion | flops 1307441152 | bytes 60950016 | tf_op jit(solution)/shard_map/thd,khd->htk/dot_general | solution.py:113
  225.1 10.8 %fusion.7 = f32[2432,1,128]{2,0,1:T(8,128)S(1)} fusion(bf16[2048,128]{1,0:T(8,128)(2,1)} %copy-done.8, f32[2048,2432]{1,0:T(8,128)} %get-tuple-element.15), kind=kOutput, calls=%fused_computation.12 | convolution fusion | flops 1280049152 | bytes 21692416 | tf_op jit(solution)/shard_map/htk,thd->khd/dot_general | solution.py:126
  235.9 13.5 %multiply_convert_fusion = bf16[2048,2432]{1,0:T(8,128)(2,1)S(1)} fusion(f32[2048,2432]{1,0:T(8,128)} %get-tuple-element.42, f32[2048,2432]{1,0:T(8,128)} %get-tuple-element.15, f32[2048]{0:T(1024)S(1)} %get-tuple-element.14), kind=kLoop, calls=%fused_computation | loop fusion | flops 19922944 | bytes 49815552 | tf_op jit(solution)/shard_map/convert_element_type | solution.py:117
  249.5 3.8 copy-done.2
  253.3 4.1 convolution_bitcast_fusion
  258.5 2.8 collective-permute-start.3
  261.3 14.5 %fusion.26 = f32[128,2048]{1,0:T(8,128)} fusion(bf16[2048,2048]{1,0:T(8,128)(2,1)} %all-gather.5.cloned.1.call-done, f32[2048,2432]{1,0:T(8,128)} %get-tuple-element.15, bf16[128,128]{1,0:T(8,128)(2,1)S(1)} %get-tuple-element.33, bf16[128,128]{1,0:T(8,128)(2,1)S(1)} %get-tuple-element.29, bf16[128,128]{1,0:T(8,128)(2,1)S(1)} %get-tuple-element.27, ...), kind=kOutput, calls=%fused_computation.41 | convolution fusion | flops 2356543488 | bytes 29982720 | tf_op jit(solution)/shard_map/dot_general | solution.py:25
  275.8 7.2 %fusion.13 = bf16[2048,128]{0,1:T(8,128)(2,1)S(1)} fusion(bf16[2048,2432]{1,0:T(8,128)(2,1)} %copy-done.2, bf16[128,128]{1,0:T(8,128)(2,1)S(1)} %get-tuple-element.32, bf16[128,128]{1,0:T(8,128)(2,1)S(1)} %get-tuple-element.28, bf16[128,128]{1,0:T(8,128)(2,1)S(1)} %get-tuple-element.26, bf16[2048,128]{1,0:T(8,128)(2,1)S(1)} %get-tuple-element.39), kind=kOutput, calls=%fused_computation.23 | convolution fusion | flops 1277820928 | bytes 11108352 | tf_op jit(solution)/shard_map/htk,khd->thd/dot_general | solution.py:119
  283.8 8.1 %fusion.48 = f32[2048,2048]{1,0:T(8,128)} fusion(bf16[2048,128]{0,1:T(8,128)(2,1)S(1)} %fusion.13, bf16[2048,128]{1,0:T(8,128)(2,1)S(1)} %copy-done.7), kind=kOutput, calls=%fused_computation.100 | convolution fusion | flops 1073741824 | bytes 17825792 | tf_op jit(solution)/shard_map/dot_general | solution.py:31
  292.0 4.5 collective-permute-start.5
  303.7 8.3 %fusion.49 = f32[2048,2048]{1,0:T(8,128)} fusion(bf16[2048,128]{1,0:T(8,128)(2,1)S(1)} %fusion.24, bf16[2048,128]{1,0:T(8,128)(2,1)S(1)} %copy-done), kind=kOutput, calls=%fused_computation.101 | convolution fusion | flops 1073741824 | bytes 17825792 | tf_op jit(solution)/shard_map/dot_general | solution.py:31
  312.0 18.6 %add_add_fusion = f32[2048,2048]{1,0:T(8,128)} fusion(f32[2048,2048]{1,0:T(8,128)} %fusion.48, f32[2048,2048]{1,0:T(8,128)} %fusion.49, bf16[2048,128]{1,0:T(8,128)(2,1)S(1)} %fusion.20, bf16[2048,128]{1,0:T(8,128)(2,1)S(1)} %copy-done.5), kind=kOutput, calls=%fused_computation.5 | convolution fusion | flops 1082130432 | bytes 51380224 | tf_op jit(solution)/shard_map/dot_general | solution.py:31
  330.6 42.0 %all-reduce.3.cloned.1.call-done = (f32[2048,128]{0,1:T(8,128)}, f32[2048,128]{0,1:T(8,128)}, f32[2048,128]{0,1:T(8,128)}, f32[128,2048]{1,0:T(8,128)}) async-done(((f32[2048,128]{0,1:T(8,128)}, f32[2048,128]{0,1:T(8,128)}, f32[2048,128]{0,1:T(8,128)}, f32[128,2048]{1,0:T(8,128)}), (f32[2048,128]{0,1:T(8,128)}, f32[2048,128]{0,1:T(8,128)}, f32[2048,128]{0,1:T(8,128)}, ...) | async-done | bytes 4194320 | tf_op jit(solution)/shard_map/psum | solution.py:162
  372.6 2.5 copy.13
  375.2 2.5 copy.14
  377.7 2.5 copy.15
  380.2 107.8 %reduce-scatter.2.cloned.1.call-done = f32[2048,128]{1,0:T(8,128)} async-done(((f32[2048,2048]{1,0:T(8,128)}), f32[2048,128]{1,0:T(8,128)}) %reduce-scatter.2.cloned.1.call-update) | async-done | bytes 1048592 | tf_op jit(solution)/shard_map/reduce_scatter | solution.py:176
  (81 shorter events, 27.6 us)
Async XLA Ops:
  7.2 90.2 %copy-start = (bf16[2048,128]{1,0:T(8,128)(2,1)S(1)}, bf16[2048,128]{1,0:T(8,128)(2,1)}, u32[]{:S(2)}) copy-start(bf16[2048,128]{1,0:T(8,128)(2,1)} %param.9) | copy-start | bytes 1572868
  7.2 83.8 %all-gather.3.cloned.1.call-start = ((), (), s32[]{:S(2)}) async-start(), calls=%async_computation.1 | async-start | bytes 8912896 | tf_op jit(solution)/shard_map/all_gather | solution.py:52
  7.9 163.0 %all-gather.5.cloned.1.call-start = ((), (), s32[]{:S(2)}) async-start(), calls=%async_computation.2 | async-start | bytes 8912896 | tf_op jit(solution)/shard_map/all_gather | solution.py:110
  8.7 364.0 %all-reduce.3.cloned.1.call-start = ((), (), s32[]{:S(2)}) async-start(), calls=%async_computation.4 | async-start | bytes 8388608 | tf_op jit(solution)/shard_map/psum | solution.py:162
  91.0 6.3 %copy-start.1 = (bf16[2048,2048]{1,0:T(8,128)(2,1)S(1)}, bf16[2048,2048]{1,0:T(8,128)(2,1)}, u32[]{:S(2)}) copy-start(bf16[2048,2048]{1,0:T(8,128)(2,1)} %all-gather.3.cloned.1.call-done) | copy-start | bytes 25165828
  96.9 4.9 copy-start.6
  100.2 76.5 %collective-permute-start = (bf16[2,224,128]{2,1,0:T(8,128)(2,1)S(1)}, bf16[2,224,128]{2,1,0:T(8,128)(2,1)S(1)}, u32[]{:S(2)}, u32[]{:S(2)}) collective-permute-start(bf16[2,224,128]{2,1,0:T(8,128)(2,1)S(1)} %maximum_maximum_fusion), channel_id=1, source_target_pairs={{0,16},{16,0},{32,48},{48,32},{64,80},{80,64},{96,112},{112,96},{1... | collective-permute-start | bytes 344072 | tf_op jit(solution)/shard_map/ppermute | solution.py:15
  104.2 81.3 %copy-start.9 = (f32[2432]{0:T(1024)S(1)}, f32[2432]{0:T(1024)}, u32[]{:S(2)}) copy-start(f32[2432]{0:T(1024)} %constant.38.clone.1) | copy-start | bytes 29188
  176.7 27.8 %copy-start.8 = (bf16[2048,128]{1,0:T(8,128)(2,1)}, bf16[2048,128]{1,0:T(8,128)(2,1)S(1)}, u32[]{:S(2)}) copy-start(bf16[2048,128]{1,0:T(8,128)(2,1)S(1)} %convolution_convert_fusion) | copy-start | bytes 1572868
  176.8 3.5 collective-permute-start.1
  180.4 5.2 %collective-permute-start.2 = (bf16[2,128,128]{2,1,0:T(8,128)(2,1)S(1)}, bf16[2,128,128]{2,1,0:T(8,128)(2,1)S(1)}, u32[]{:S(2)}, u32[]{:S(2)}) collective-permute-start(bf16[2,128,128]{2,1,0:T(8,128)(2,1)S(1)} %maximum_select_fusion.1), channel_id=1, source_target_pairs={{0,64},{16,80},{32,96},{48,112},{64,0},{80,16},{96,32},{112,48},{1... | collective-permute-start | bytes 196616 | tf_op jit(solution)/shard_map/ppermute | solution.py:15
  249.5 3.8 copy-start.2
  257.4 1.0 copy-start.3
  258.5 24.6 %collective-permute-start.3 = (f32[2,128,128]{2,1,0:T(8,128)S(1)}, f32[2,128,128]{2,1,0:T(8,128)S(1)}, u32[]{:S(2)}, u32[]{:S(2)}) collective-permute-start(f32[2,128,128]{2,1,0:T(8,128)S(1)} %pad_maximum_fusion.4), channel_id=1, source_target_pairs={{0,64},{16,80},{32,96},{48,112},{64,0},{80,16},{96,32},{112,48},{1... | collective-permute-start | bytes 393224 | tf_op jit(solution)/shard_map/ppermute | solution.py:15
  275.8 7.9 %copy-start.7 = (bf16[2048,128]{1,0:T(8,128)(2,1)S(1)}, bf16[2048,128]{1,0:T(8,128)(2,1)}, u32[]{:S(2)}) copy-start(bf16[2048,128]{1,0:T(8,128)(2,1)} %param.8) | copy-start | bytes 1572868
  283.1 13.3 %slice-start = ((s8[8388608]{0:T(1024)(128)(4,1)}), s8[4194304]{0:T(1024)(128)(4,1)S(1)}, s32[]{:S(2)}) async-start(s8[8388608]{0:T(1024)(128)(4,1)} %bitcast.147), calls=%async_computation.5 | async-start | bytes 8388608
  283.2 13.3 %slice-start.1 = ((s8[8388608]{0:T(1024)(128)(4,1)}), s8[4194304]{0:T(1024)(128)(4,1)S(1)}, s32[]{:S(2)}) async-start(s8[8388608]{0:T(1024)(128)(4,1)} %bitcast.147), calls=%async_computation.6 | async-start | bytes 8388608
  283.2 8.7 %collective-permute-start.4 = (f32[2,192,128]{2,1,0:T(8,128)S(1)}, f32[2,192,128]{2,1,0:T(8,128)S(1)}, u32[]{:S(2)}, u32[]{:S(2)}) collective-permute-start(f32[2,192,128]{2,1,0:T(8,128)S(1)} %pad_maximum_fusion.3), channel_id=1, source_target_pairs={{0,32},{16,48},{32,0},{48,16},{64,96},{80,112},{96,64},{112,80},{1... | collective-permute-start | bytes 589832 | tf_op jit(solution)/shard_map/ppermute | solution.py:15
  291.9 6.9 %copy-start.4 = (f32[2432,1,128]{2,0,1:T(8,128)S(1)}, f32[2432,1,128]{2,0,1:T(8,128)}, u32[]{:S(2)}) copy-start(f32[2432,1,128]{2,0,1:T(8,128)} %copy-done.3) | copy-start | bytes 3735556
  292.0 6.7 %collective-permute-start.5 = (f32[2,224,128]{2,1,0:T(8,128)S(1)}, f32[2,224,128]{2,1,0:T(8,128)S(1)}, u32[]{:S(2)}, u32[]{:S(2)}) collective-permute-start(f32[2,224,128]{2,1,0:T(8,128)S(1)} %pad_maximum_fusion.2), channel_id=1, source_target_pairs={{0,16},{16,0},{32,48},{48,32},{64,80},{80,64},{96,112},{112,96},{1... | collective-permute-start | bytes 688136 | tf_op jit(solution)/shard_map/ppermute | solution.py:15
  303.7 8.4 %copy-start.5 = (bf16[2048,128]{1,0:T(8,128)(2,1)S(1)}, bf16[2048,128]{1,0:T(8,128)(2,1)}, u32[]{:S(2)}) copy-start(bf16[2048,128]{1,0:T(8,128)(2,1)} %param.10) | copy-start | bytes 1572868
  303.7 184.4 %reduce-scatter.2.cloned.1.call-start = ((), (), s32[]{:S(2)}) async-start(), calls=%async_computation.3 | async-start | bytes 17825792 | tf_op jit(solution)/shard_map/reduce_scatter | solution.py:176
Sparse Core Ops, SparseCore 0:
  10.1 80.8 all-gather.2
  93.1 77.7 all-gather.4
  303.8 68.7 all-reduce.2
  375.9 112.0 reduce-scatter.1
where the time goes:
time: 507 us; the launch traced here: 499 us
  waiting for transfers between devices  304 us (60%)
  matrix products  124 us (24%)
  other arithmetic  27.6 us (5%)
  local copies, waits for them, and re-layouts  14.8 us (3%)
  between operations  14.4 us (3%)
  starting transfers between devices  14.2 us (3%)
    reduce_scatter x1, waiting for transfers between devices, body(): lax.psum_scatter(partial_grad, 'tp', scatter_dimension=1, tiled=True)  108 us
    all_gather x1, waiting for transfers between devices, body(): feats = lax.all_gather(tokens, 'tp', axis=1, tiled=True)  82.3 us
    all_gather x1, waiting for transfers between devices, body(): dy_full = lax.all_gather(cotangent, 'tp', axis=1, tiled=True)  66.6 us
    psum x1, waiting for transfers between devices, body(): lax.psum((contract_rows(feats, d_queries), contract_rows(feats, d_keys),...  42 us
    dot_general x4, matrix products, contract_cols(): lax.dot_general(left, right, (((1,), (1,)), ((), ())), preferred_element_...  40.8 us
    dot_general x4, matrix products, contract_rows(): lax.dot_general(left, right, (((0,), (0,)), ((), ())), preferred_element_...  21.3 us
    dot_general x1, matrix products, body(): jnp.einsum('thd,khd->htk', d_att_heads, value_heads, preferred_element_ty...  20.6 us
    unnamed x28, local copies, waits for them, and re-layouts  14.7 us
  transfers between devices with their start and end apart: 10, of which 6 were waited for; matrix products, arithmetic and copies ran while one was open for 17% of the time, Pallas kernels for 0%

commit v1 on v0

v1 whole, which is shorter than its diff:
```python
import functools
import math

import jax
import jax.numpy as jnp
from jax import lax
from jax.experimental import pallas as pl
from jax.experimental.pallas import tpu as pltpu
from jax.sharding import PartitionSpec as P

DH = 128
RATIO = 16
NX = 4
NZ = 4
NY = 4
BF = jnp.bfloat16
F32 = jnp.float32
STEPS = (0, 1, -1, 2)
LOG2E = 1.0 / math.log(2.0)
NT = (((1,), (1,)), ((), ()))
NN = (((1,), (0,)), ((), ()))


def mm(a, b, dims=NN):
    return lax.dot_general(a, b, dims, preferred_element_type=F32)


def place(ctx, first, second):
    x, z = (first, second) if ctx % 2 == 0 else (second, first)
    return ctx * NX * NZ + x * NZ + z


def send(value, first, second):
    pairs = [
        (place(ctx, a, b), place(ctx, (a + first) % NX, (b + second) % NZ))
        for ctx in range(NY * 2)
        for a in range(NX)
        for b in range(NZ)
    ]
    return lax.ppermute(value, ("ctx", "tp"), pairs)


def first_lines():
    return [
        [place(ctx, a, b) for a in range(NX)] for ctx in range(NY * 2) for b in range(NZ)
    ]


def position():
    me = lax.axis_index("tp")
    x, z = me // NZ, me % NZ
    even = lax.axis_index("ctx") % 2 == 0
    return even, jnp.where(even, x, z), jnp.where(even, z, x)


def send_core(value):
    return lax.ppermute(value, "ctx", [(i, i ^ 1) for i in range(NY * 2)])


def order_kernel(x_ref, dep_ref, out_ref):
    pass


def after(value, dep):
    return pl.pallas_call(
        order_kernel,
        in_specs=[pl.BlockSpec(memory_space=pl.ANY)] * 2,
        out_specs=pl.BlockSpec(memory_space=pl.ANY),
        out_shape=jax.ShapeDtypeStruct(value.shape, value.dtype),
        input_output_aliases={0: 0},
    )(value, dep)


def gather_features(block):
    up, down, far = [send(block, step, 0) for step in STEPS[1:]]
    near, rest = jnp.stack([block, up]), jnp.stack([down, far])
    near, rest = after(near, rest), after(rest, near)
    near_up, rest_down = send(near, 0, 1), send(rest, 0, -1)
    near_down, rest_up = send(near, 0, -1), send(rest, 0, 1)
    near_far, rest_far = send(near_up, 0, 1), send(rest_down, 0, -1)
    return [near, rest, near_up, rest_up, near_down, rest_down, near_far, rest_far]


def block_ids():
    even, first, second = position()
    ids = []
    for b in STEPS:
        for a in STEPS:
            i, j = (first - a) % NX, (second - b) % NZ
            ids.append(jnp.where(even, i * NZ + j, j * NZ + i))
    return jnp.stack(ids).astype(jnp.int32)


def project_kernel(ids, *refs):
    parts = refs[:8]
    w_ref, full_ref, q_ref, kv_ref = refs[8:12]
    pooled = refs[12:]
    for i in range(16):
        start = pl.multiple_of(ids[i] * 128, 128)
        full_ref[:, pl.ds(start, 128)] = parts[i // 2][i % 2]
    out = mm(full_ref[...], w_ref[...]).astype(BF)
    q_ref[...] = out[:, :DH]
    kv = out[:, DH:]
    kv_ref[...] = kv
    rows = kv.shape[0]
    for l, ref in enumerate(pooled):
        width = RATIO * 2**l
        window = lax.broadcasted_iota(jnp.int32, (rows // width, rows), 0)
        row = lax.broadcasted_iota(jnp.int32, (rows // width, rows), 1)
        inside = jnp.where((row >= window * width) & (row < (window + 1) * width), 1.0, 0.0)
        ref[...] = mm(inside.astype(BF), kv) * (1.0 / width)


def project(ids, parts, weight, levels):
    n = parts[0].shape[1]
    feats = 16 * 128
    rows = 512
    row_map = lambda i, ids: (i, 0)
    pooled = [n // (RATIO * 2**l) for l in range(levels)]
    return pl.pallas_call(
        project_kernel,
        grid_spec=pltpu.PrefetchScalarGridSpec(
            num_scalar_prefetch=1,
            grid=(n // rows,),
            in_specs=[pl.BlockSpec((2, rows, 128), lambda i, ids: (0, i, 0))] * 8
            + [pl.BlockSpec(weight.shape, lambda i, ids: (0, 0))],
            out_specs=[
                pl.BlockSpec((rows, feats), row_map),
                pl.BlockSpec((rows, DH), row_map),
                pl.BlockSpec((rows, 2 * DH), row_map),
            ]
            + [pl.BlockSpec((p * rows // n, 2 * DH), row_map) for p in pooled],
        ),
        out_shape=[
            jax.ShapeDtypeStruct((n, feats), BF),
            jax.ShapeDtypeStruct((n, DH), BF),
            jax.ShapeDtypeStruct((n, 2 * DH), BF),
        ]
        + [jax.ShapeDtypeStruct((p, 2 * DH), F32) for p in pooled],
        compiler_params=pltpu.CompilerParams(vmem_limit_bytes=60 * 2**20),
        cost_estimate=pl.CostEstimate(
            flops=6 * n * feats * DH, bytes_accessed=4 * n * feats, transcendentals=0
        ),
    )(ids, *parts, weight)


def add_bias(scores, own, coarse):
    out = [scores[:own]]
    for l in range((scores.shape[0] - own) // coarse):
        low = own + l * coarse
        out.append(scores[low : low + coarse] + math.log(RATIO * 2**l) * LOG2E)
    return jnp.concatenate(out, axis=0)


def forward_kernel(own, coarse, q_ref, kv_ref, sib_ref, att_ref, lse_ref, k_ref, vt_ref):
    @pl.when(pl.program_id(0) == 0)
    def _():
        k_ref[:own] = kv_ref[:, :DH]
        k_ref[own:] = sib_ref[:, :DH]
        vt_ref[:, :own] = kv_ref[:, DH:].T
        vt_ref[:, own:] = sib_ref[:, DH:].T

    scores = mm(k_ref[...], q_ref[...], NT) * (DH**-0.5 * LOG2E)
    scores = add_bias(scores, own, coarse)
    peak = jnp.max(scores, axis=0, keepdims=True)
    expo = jnp.exp2(scores - peak)
    total = jnp.sum(expo, axis=0, keepdims=True)
    probs = (expo * (1.0 / total)).astype(BF)
    att_ref[...] = mm(vt_ref[...], probs).astype(BF)
    lse_ref[...] = peak + jnp.log2(total)


def attend(queries, listed, siblings, coarse):
    n = queries.shape[0]
    own, more = listed.shape[0], siblings.shape[0]
    m = own + more
    rows = 256
    whole = lambda i: (0, 0)
    return pl.pallas_call(
        functools.partial(forward_kernel, own, coarse),
        grid=(n // rows,),
        in_specs=[
            pl.BlockSpec((rows, DH), lambda i: (i, 0)),
            pl.BlockSpec((own, 2 * DH), whole),
            pl.BlockSpec((more, 2 * DH), whole),
        ],
        out_specs=[
            pl.BlockSpec((DH, rows), lambda i: (0, i)),
            pl.BlockSpec((1, rows), lambda i: (0, i)),
        ],
        out_shape=[
            jax.ShapeDtypeStruct((DH, n), BF),
            jax.ShapeDtypeStruct((1, n), F32),
        ],
        scratch_shapes=[pltpu.VMEM((m, DH), BF), pltpu.VMEM((DH, m), BF)],
        compiler_params=pltpu.CompilerParams(vmem_limit_bytes=60 * 2**20),
        cost_estimate=pl.CostEstimate(
            flops=8 * n * m * DH, bytes_accessed=4 * n * DH, transcendentals=n * m
        ),
    )(queries, listed, siblings)


def backward_kernel(
    own, coarse, q_ref, kv_ref, sib_ref, cot_ref, wo_ref, lse_ref,
    dq_ref, dkv_ref, dsib_ref, k_ref, v_ref, kt_ref, acc_ref,
):
    step = pl.program_id(0)

    @pl.when(step == 0)
    def _():
        k_ref[:own] = kv_ref[:, :DH]
        k_ref[own:] = sib_ref[:, :DH]
        v_ref[:own] = kv_ref[:, DH:]
        v_ref[own:] = sib_ref[:, DH:]
        kt_ref[...] = k_ref[...].T
        acc_ref[...] = jnp.zeros_like(acc_ref)

    q = q_ref[...]
    da = mm(cot_ref[...], wo_ref[...], NT).astype(BF)
    scores = mm(k_ref[...], q, NT) * (DH**-0.5 * LOG2E)
    probs = jnp.exp2(add_bias(scores, own, coarse) - lse_ref[...])
    d_probs = mm(v_ref[...], da, NT)
    delta = jnp.sum(probs * d_probs, axis=0, keepdims=True)
    d_scores = (DH**-0.5 * probs * (d_probs - delta)).astype(BF)
    probs = probs.astype(BF)
    acc_ref[:, :DH] += mm(d_scores, q)
    acc_ref[:, DH:] += mm(probs, da)
    dq_ref[...] = mm(kt_ref[...], d_scores).T.astype(BF)

    @pl.when(step == pl.num_programs(0) - 1)
    def _():
        dkv_ref[...] = acc_ref[:own]
        dsib_ref[...] = acc_ref[own:]


def attend_back(queries, listed, siblings, cot, w_out, lse, coarse):
    n, feats = cot.shape
    own, more = listed.shape[0], siblings.shape[0]
    m = own + more
    rows = 256
    whole = lambda i: (0, 0)
    return pl.pallas_call(
        functools.partial(backward_kernel, own, coarse),
        grid=(n // rows,),
        in_specs=[
            pl.BlockSpec((rows, DH), lambda i: (i, 0)),
            pl.BlockSpec((own, 2 * DH), whole),
            pl.BlockSpec((more, 2 * DH), whole),
            pl.BlockSpec((rows, feats), lambda i: (i, 0)),
            pl.BlockSpec((DH, feats), whole),
            pl.BlockSpec((1, rows), lambda i: (0, i)),
        ],
        out_specs=[
            pl.BlockSpec((rows, DH), lambda i: (i, 0)),
            pl.BlockSpec((own, 2 * DH), whole),
            pl.BlockSpec((more, 2 * DH), whole),
        ],
        out_shape=[
            jax.ShapeDtypeStruct((n, DH), BF),
            jax.ShapeDtypeStruct((own, 2 * DH), F32),
            jax.ShapeDtypeStruct((more, 2 * DH), F32),
        ],
        scratch_shapes=[
            pltpu.VMEM((m, DH), BF),
            pltpu.VMEM((m, DH), BF),
            pltpu.VMEM((DH, m), BF),
            pltpu.VMEM((m, 2 * DH), F32),
        ],
        compiler_params=pltpu.CompilerParams(vmem_limit_bytes=60 * 2**20),
        cost_estimate=pl.CostEstimate(
            flops=20 * n * m * DH, bytes_accessed=2 * n * feats, transcendentals=n * m
        ),
    )(queries, listed, siblings, cot, w_out, lse)


def token_grad_kernel(ids, d_ref, *refs):
    weights, outs = refs[:NZ], refs[NZ:]
    d = jnp.concatenate([d_ref[i] for i in range(NX)], axis=1)
    w = jnp.concatenate([w[...].reshape(d.shape[1], DH) for w in weights], axis=1)
    out = mm(d, w)
    for step in range(NZ):
        outs[step][0] = out[:, step * DH : (step + 1) * DH]


def token_grad_parts(d_rows, weights):
    heads, rows, cols = d_rows.shape
    even, _, second = position()
    ids = []
    for i in range(NX):
        for step in range(NZ):
            j = (second + step) % NZ
            ids.append(jnp.where(even, i * NZ + j, j * NZ + i))
    ids = jnp.stack(ids).astype(jnp.int32)

    def column(step):
        return pl.BlockSpec((heads, cols, DH), lambda i, ids: (0, 0, ids[i * NZ + step]))

    return pl.pallas_call(
        token_grad_kernel,
        grid_spec=pltpu.PrefetchScalarGridSpec(
            num_scalar_prefetch=1,
            grid=(NX,),
            in_specs=[pl.BlockSpec((heads, rows, cols), lambda i, ids: (0, 0, 0))]
            + [column(step) for step in range(NZ)],
            out_specs=[pl.BlockSpec((1, rows, DH), lambda i, ids: (i, 0, 0))] * NZ,
        ),
        out_shape=[jax.ShapeDtypeStruct((NX, rows, DH), F32)] * NZ,
        compiler_params=pltpu.CompilerParams(vmem_limit_bytes=60 * 2**20),
        cost_estimate=pl.CostEstimate(
            flops=2 * heads * rows * cols * 2048,
            bytes_accessed=2 * heads * cols * 2048 + 8192 * rows,
            transcendentals=0,
        ),
    )(ids, d_rows, weights, weights, weights, weights)


def weight_grad_kernel(x_ref, d_ref, *refs):
    outs, dt_ref = refs[:-1], refs[-1]

    @pl.when(pl.program_id(0) == 0)
    def _():
        dt_ref[...] = d_ref[...].T

    grads = mm(dt_ref[...], x_ref[...]).T
    for i, out_ref in enumerate(outs):
        out_ref[...] = grads[:, i * DH : (i + 1) * DH]


def weight_grads(feats, grads):
    n, f = feats.shape
    count = grads.shape[1] // DH
    cols = 512
    return pl.pallas_call(
        weight_grad_kernel,
        grid=(f // cols,),
        in_specs=[
            pl.BlockSpec((n, cols), lambda i: (0, i)),
            pl.BlockSpec(grads.shape, lambda i: (0, 0)),
        ],
        out_specs=[pl.BlockSpec((cols, DH), lambda i: (i, 0))] * count,
        out_shape=[jax.ShapeDtypeStruct((f, DH), F32)] * count,
        scratch_shapes=[pltpu.VMEM((count * DH, n), BF)],
        compiler_params=pltpu.CompilerParams(vmem_limit_bytes=60 * 2**20),
        cost_estimate=pl.CostEstimate(
            flops=2 * n * f * DH * count,
            bytes_accessed=2 * n * f + 4 * f * DH * count,
            transcendentals=0,
        ),
    )(feats, grads)


def sibling_rows():
    me = lax.axis_index("ctx")
    return ((me >> 1) ^ 1) * 2, ((me >> 2) ^ 1) * 4


def fetch_pooled(pooled):
    half = pooled[1].shape[0]
    me = lax.axis_index("ctx")
    third = jnp.concatenate([pooled[2], pooled[2]], axis=0)
    buffer = jnp.stack([jnp.where((me ^ d) >= 4, third, pooled[1]) for d in range(NY * 2)])
    got = lax.all_to_all(buffer, "ctx", 0, 0)
    second, last = sibling_rows()
    cols = buffer.shape[2]
    level1 = lax.dynamic_slice_in_dim(got, second, 2, 0).reshape(2 * half, cols)
    level2 = lax.dynamic_slice_in_dim(got, last, 4, 0)[:, : half // 2].reshape(2 * half, cols)
    return [send_core(pooled[0]), level1, level2]


def return_pooled(grads, coarse, *meanwhile):
    half, cols = coarse // 2, grads.shape[1]
    second, last = sibling_rows()
    level1 = grads[coarse : 2 * coarse].reshape(2, half, cols)
    level2 = grads[2 * coarse :].reshape(4, half // 2, cols)
    level2 = jnp.concatenate([level2, jnp.zeros_like(level2)], axis=1)
    buffer = jnp.zeros((NY * 2, half, cols), F32)
    buffer = lax.dynamic_update_slice_in_dim(buffer, level1, second, 0)
    buffer = lax.dynamic_update_slice_in_dim(buffer, level2, last, 0)
    got = lax.all_to_all(buffer, "ctx", 0, 0)
    for done in meanwhile:
        got = after(got, done)
    level1 = jnp.sum(lax.dynamic_slice_in_dim(got, second, 2, 0), axis=0)
    level2 = jnp.sum(lax.dynamic_slice_in_dim(got, last, 4, 0)[:, : half // 2], axis=0)
    return [send_core(grads[:coarse]), level1, level2]


def body(tokens, cotangent, w_query, w_key, w_value, w_out):
    own = tokens.shape[0]
    coarse = own // RATIO
    levels = 3
    ids = block_ids()
    weights = jnp.concatenate([w_query, w_key, w_value], axis=1)
    tok_parts = gather_features(tokens)
    cot = lax.all_gather(after(cotangent, tok_parts[1]), "tp", axis=1, tiled=True)
    feats, queries, keys_values, *pooled = project(ids, tok_parts, weights, levels)
    pooled = [p.astype(BF) for p in pooled]
    siblings = jnp.concatenate(fetch_pooled(pooled), axis=0)
    attended_t, lse = attend(queries, keys_values, siblings, coarse)
    lines = first_lines()
    weight_heads = lax.all_gather(
        after(weights.T, queries), ("ctx", "tp"), axis_index_groups=lines
    )

    out_part = mm(attended_t, cot)
    d_queries, total, d_siblings = attend_back(
        queries, keys_values, siblings, cot, w_out, lse, coarse
    )
    grads = return_pooled(d_siblings, coarse, out_part)
    for l in range(levels):
        width = RATIO * 2**l
        total = total + jnp.broadcast_to(
            grads[l][:, None, :] / width, (own // width, width, 2 * DH)
        ).reshape(own, 2 * DH)
    d_all = jnp.concatenate([d_queries, total.astype(BF)], axis=1)
    query_grad, key_grad, value_grad, out_grad = lax.psum(
        tuple(weight_grads(feats, d_all)) + (out_part,), "ctx"
    )
    d_rows = d_all.reshape(NX, own // NX, 3 * DH)
    d_rows = lax.all_to_all(d_rows, ("ctx", "tp"), 0, 0, axis_index_groups=lines)
    parts = token_grad_parts(d_rows, weight_heads)
    total = parts[0]
    for step in range(1, NZ):
        total = total + send(parts[step], 0, step)
    token_grad = lax.all_to_all(
        total.astype(BF), ("ctx", "tp"), 0, 0, axis_index_groups=lines
    ).reshape(own, DH)
    return (token_grad, query_grad, key_grad, value_grad, out_grad)


def solution(mesh):
    return jax.shard_map(
        body,
        mesh=mesh,
        in_specs=(
            P("ctx", "tp"),
            P("ctx", "tp"),
            P(None, "tp"),
            P(None, "tp"),
            P(None, "tp"),
            P("tp", None),
        ),
        out_specs=(P("ctx", "tp"), P(None, "tp"), P(None, "tp"), P(None, "tp"), P("tp", None)),
        check_vma=False,
    )
```

time: 507 us -> 285 us (0.56); the launches traced: 499 us -> 284 us
  waiting for transfers between devices: 304 us -> 104 us
  matrix products: 124 us -> 5.61 us
  Pallas kernels: 0 us -> 75.2 us
  starting transfers between devices: 14.2 us -> 40.5 us
  other arithmetic: 27.6 us -> 14.7 us
  blocking collectives: 0 us -> 9.33 us
  local copies, waits for them, and re-layouts: 14.8 us -> 20.1 us
    all_gather x2, waiting for transfers between devices: 149 us -> 0.01 us  [the longest x1 0.01 us: body(): lax.all_gather(after(cotangent, tok_parts[1]), 'tp', axis=1, tiled=True)]
    dot_general x16 -> x1, matrix products: 124 us -> 5.61 us  [mm(): return lax.dot_general(a, b, dims, preferred_element_type=F32)]
    reduce_scatter x1 -> x0, waiting for transfers between devices: 108 us -> none  [body(): lax.psum_scatter(partial_grad, 'tp', scatter_dimension=1, tiled=True)]
    pallas_call x0 -> x10, Pallas kernels: none -> 75.2 us  [the longest x1 28.9 us: attend_back(): pl.pallas_call(functools.partial(backward_kernel, own, coarse), grid=(n /...]
    ppermute x6 -> x14, waiting for transfers between devices: 4.14 us -> 72.8 us  [the longest x12 72.7 us: send(): return lax.ppermute(value, ('ctx', 'tp'), pairs)]
    psum x1, waiting for transfers between devices: 42 us -> 17.9 us  [body(): lax.psum(tuple(weight_grads(feats, d_all)) + (out_part,), 'ctx')]
    all_to_all x0 -> x3, starting transfers between devices: none -> 20.9 us  [the longest x1 11.7 us: fetch_pooled(): got = lax.all_to_all(buffer, 'ctx', 0, 0)]
    convert_element_type x4, other arithmetic: 15.9 us -> 1.83 us  [the longest x1 1.49 us: body(): total.astype(BF)]
  transfers between devices with their start and end apart: 10 -> 20, of which waited for: 6 -> 13; matrix products, arithmetic and copies ran while one was open for 17% -> 10% of each run, Pallas kernels for 0% -> 27%
where the time goes in v1:
time: 285 us; the launch traced here: 284 us
  waiting for transfers between devices  104 us (36%)
  Pallas kernels  75.2 us (26%)
  starting transfers between devices  40.5 us (14%)
  local copies, waits for them, and re-layouts  20.1 us (7%)
  other arithmetic  14.7 us (5%)
  between operations  14 us (5%)
  blocking collectives  9.33 us (3%)
  matrix products  5.61 us (2%)
    ppermute x12, waiting for transfers between devices, send(): return lax.ppermute(value, ('ctx', 'tp'), pairs)  72.7 us
    pallas_call x1, Pallas kernels, attend_back(): pl.pallas_call(functools.partial(backward_kernel, own, coarse), grid=(n /...  28.9 us
    ppermute x12, starting transfers between devices, send(): return lax.ppermute(value, ('ctx', 'tp'), pairs)  19.1 us
    psum x1, waiting for transfers between devices, body(): lax.psum(tuple(weight_grads(feats, d_all)) + (out_part,), 'ctx')  17.9 us
    pallas_call x1, Pallas kernels, attend(): pl.pallas_call(functools.partial(forward_kernel, own, coarse), grid=(n //...  16.4 us
    unnamed x44, local copies, waits for them, and re-layouts  14 us
    pallas_call x1, Pallas kernels, project(): pl.pallas_call(project_kernel, grid_spec=pltpu.PrefetchScalarGridSpec(num...  12.5 us
    all_to_all x1, starting transfers between devices, fetch_pooled(): got = lax.all_to_all(buffer, 'ctx', 0, 0)  11.7 us
  transfers between devices with their start and end apart: 20, of which 13 were waited for; matrix products, arithmetic and copies ran while one was open for 10% of the time, Pallas kernels for 27%

profile of v1, /device:TPU:1, one launch (start us, length us, event | category | flops | bytes accessed | tf_op | source)
XLA Modules:
  0.0 283.7 jit_solution(10898725007102784072)
XLA Ops:
  9.1 4.4 %collective-permute-start.2 = (bf16[2048,128]{1,0:T(8,128)(2,1)}, bf16[2048,128]{1,0:T(8,128)(2,1)S(1)}, u32[]{:S(2)}, u32[]{:S(2)}) collective-permute-start(bf16[2048,128]{1,0:T(8,128)(2,1)} %param.6), channel_id=1, source_target_pairs={{0,8},{1,9},{2,10},{3,11},{4,12},{5,13},{6,14},{7,15},{8,0},{9,1},... | collective-permute-start | bytes 1572872 | tf_op jit(solution)/shard_map/ppermute | solution.py:40
  15.0 5.6 %collective-permute-done.2 = bf16[2048,128]{1,0:T(8,128)(2,1)S(1)} collective-permute-done((bf16[2048,128]{1,0:T(8,128)(2,1)}, bf16[2048,128]{1,0:T(8,128)(2,1)S(1)}, u32[]{:S(2)}, u32[]{:S(2)}) %collective-permute-start.2) | collective-permute-done | bytes 524320 | tf_op jit(solution)/shard_map/ppermute | solution.py:40
  20.6 6.2 %collective-permute-done.1 = bf16[2048,128]{1,0:T(8,128)(2,1)S(1)} collective-permute-done((bf16[2048,128]{1,0:T(8,128)(2,1)}, bf16[2048,128]{1,0:T(8,128)(2,1)S(1)}, u32[]{:S(2)}, u32[]{:S(2)}) %collective-permute-start.1) | collective-permute-done | bytes 524320 | tf_op jit(solution)/shard_map/ppermute | solution.py:40
  35.3 9.4 %collective-permute-done.3.refs_2_ = bf16[2,2048,128]{2,1,0:T(8,128)(2,1)} collective-permute-done((bf16[2,2048,128]{2,1,0:T(8,128)(2,1)}, bf16[2,2048,128]{2,1,0:T(8,128)(2,1)}, u32[]{:S(2)}, u32[]{:S(2)}) %collective-permute-start.3) | collective-permute-done | bytes 1048608 | tf_op jit(solution)/shard_map/ppermute | solution.py:40
  47.2 3.5 %collective-permute-start.8 = (bf16[2,2048,128]{2,1,0:T(8,128)(2,1)}, bf16[2,2048,128]{2,1,0:T(8,128)(2,1)}, u32[]{:S(2)}, u32[]{:S(2)}) collective-permute-start(bf16[2,2048,128]{2,1,0:T(8,128)(2,1)} %collective-permute-done.6.refs_5_), channel_id=1, source_target_pairs={{0,3},{1,0},{2,1},{3,2},{4,7},{5,4},{6,5},{7,6},{8,11},{9,8},{10,9... | collective-permute-start | bytes 3145736 | tf_op jit(solution)/shard_map/ppermute | solution.py:40
  57.8 6.5 %collective-permute-done.4.refs_3_ = bf16[2,2048,128]{2,1,0:T(8,128)(2,1)} collective-permute-done((bf16[2,2048,128]{2,1,0:T(8,128)(2,1)S(1)}, bf16[2,2048,128]{2,1,0:T(8,128)(2,1)}, u32[]{:S(2)}, u32[]{:S(2)}) %collective-permute-start.4) | collective-permute-done | bytes 1048608 | tf_op jit(solution)/shard_map/ppermute | solution.py:40
  64.4 11.2 %collective-permute-done.7.refs_6_ = bf16[2,2048,128]{2,1,0:T(8,128)(2,1)} collective-permute-done((bf16[2,2048,128]{2,1,0:T(8,128)(2,1)}, bf16[2,2048,128]{2,1,0:T(8,128)(2,1)}, u32[]{:S(2)}, u32[]{:S(2)}) %collective-permute-start.7) | collective-permute-done | bytes 1048608 | tf_op jit(solution)/shard_map/ppermute | solution.py:40
  75.6 5.9 %collective-permute-done.8.refs_7_ = bf16[2,2048,128]{2,1,0:T(8,128)(2,1)} collective-permute-done((bf16[2,2048,128]{2,1,0:T(8,128)(2,1)}, bf16[2,2048,128]{2,1,0:T(8,128)(2,1)}, u32[]{:S(2)}, u32[]{:S(2)}) %collective-permute-start.8) | collective-permute-done | bytes 1048608 | tf_op jit(solution)/shard_map/ppermute | solution.py:40
  81.5 12.5 %shard_map.103 = (bf16[2048,2048]{1,0:T(8,128)(2,1)}, bf16[2048,128]{1,0:T(8,128)(2,1)}, bf16[2048,256]{1,0:T(8,128)(2,1)}, f32[128,256]{1,0:T(8,128)}, f32[64,256]{1,0:T(8,128)}, /*index=5*/f32[32,256]{1,0:T(8,128)}) custom-call(s32[16]{0:T(128)} %stack.180.ids, bf16[2,2048,128]{2,1,0:T(8,128)(2,1)} %shard_map.101.refs_0_, ...), custom_call_target="tpu_custom_call" | custom-call | flops 3221225472 | bytes 16777216 | tf_op jit(solution)/shard_map/pallas_call | solution.py:120
  99.9 11.7 %all-to-all-start = ((bf16[8,64,256]{2,1,0:T(8,128)(2,1)}), bf16[8,64,256]{2,1,0:T(8,128)(2,1)S(1)}, u32[]{:S(2)}, u32[]{:S(2)}) async-start(bf16[8,64,256]{2,1,0:T(8,128)(2,1)} %bitcast_dynamic-update-slice_fusion), calls=%async_computation | async-start | bytes 524288 | tf_op jit(solution)/shard_map/all_to_all | solution.py:362
  112.0 6.2 %all-to-all-done = bf16[8,64,256]{2,1,0:T(8,128)(2,1)S(1)} async-done(((bf16[8,64,256]{2,1,0:T(8,128)(2,1)}), bf16[8,64,256]{2,1,0:T(8,128)(2,1)S(1)}, u32[]{:S(2)}, u32[]{:S(2)}) %all-to-all-start) | async-done | bytes 262176 | tf_op jit(solution)/shard_map/all_to_all | solution.py:362
  118.9 16.4 %shard_map.105 = (bf16[128,2048]{1,0:T(8,128)(2,1)}, f32[1,2048]{1,0:T(1,128)}) custom-call(bf16[2048,128]{1,0:T(8,128)(2,1)} %get-tuple-element.23.q_ref.dep_ref, bf16[2048,256]{1,0:T(8,128)(2,1)} %get-tuple-element.24.kv_ref, bf16[384,256]{1,0:T(8,128)(2,1)} %pad_maximum_fusion.4.sib_ref), custom_call_target="tpu_custom_call" | custom-call | flops 5100273664 | bytes 1048576 | tf_op jit(solution)/shard_map/pallas_call | solution.py:179
  135.3 28.9 %shard_map.106 = (bf16[2048,128]{1,0:T(8,128)(2,1)}, f32[2048,256]{1,0:T(8,128)}, f32[384,256]{1,0:T(8,128)}) custom-call(bf16[2048,128]{1,0:T(8,128)(2,1)} %get-tuple-element.23.q_ref.dep_ref, bf16[2048,256]{1,0:T(8,128)(2,1)} %get-tuple-element.24.kv_ref, bf16[384,256]{1,0:T(8,128)(2,1)} %pad_maximum_fusion.4.sib_ref, ...), custom_call_target="tpu_custom_call" | custom-call | flops 12750684160 | bytes 8388608 | tf_op jit(solution)/shard_map/pallas_call | solution.py:242
  167.6 4.4 %all-to-all-start.1 = ((f32[8,64,256]{2,1,0:T(8,128)}), f32[8,64,256]{2,1,0:T(8,128)S(1)}, u32[]{:S(2)}, u32[]{:S(2)}) async-start(f32[8,64,256]{2,1,0:T(8,128)} %pad_dynamic-update-slice_fusion), calls=%async_computation.1 | async-start | bytes 1048576 | tf_op jit(solution)/shard_map/all_to_all | solution.py:379
  172.2 5.6 %fusion.3.dep_ref = f32[128,2048]{1,0:T(8,128)} fusion(bf16[128,2048]{1,0:T(8,128)(2,1)S(1)} %copy-done.5, bf16[2048,2048]{1,0:T(8,128)(2,1)} %all-gather.4.cloned.1.call-done.cot_ref), kind=kOutput, calls=%fused_computation.30 | convolution fusion | flops 1073741824 | bytes 9961472 | tf_op jit(solution)/shard_map/dot_general | solution.py:25
  177.9 3.7 %all-to-all-done.1.x_ref = f32[8,64,256]{2,1,0:T(8,128)S(1)} async-done(((f32[8,64,256]{2,1,0:T(8,128)}), f32[8,64,256]{2,1,0:T(8,128)S(1)}, u32[]{:S(2)}, u32[]{:S(2)}) %all-to-all-start.1) | async-done | bytes 524320 | tf_op jit(solution)/shard_map/all_to_all | solution.py:379
  186.0 4.7 %all-to-all-start.2 = ((bf16[4,512,384]{2,1,0:T(8,128)(2,1)}), bf16[4,512,384]{2,1,0:T(8,128)(2,1)S(1)}, u32[]{:S(2)}, u32[]{:S(2)}) async-start(bf16[4,512,384]{2,1,0:T(8,128)(2,1)} %bitcast.51), calls=%async_computation.2 | async-start | bytes 3145728 | tf_op jit(solution)/shard_map/all_to_all | solution.py:419
  190.7 8.7 %shard_map.110 = (f32[2048,128]{1,0:T(8,128)}, f32[2048,128]{1,0:T(8,128)}, f32[2048,128]{1,0:T(8,128)}) custom-call(bf16[2048,2048]{1,0:T(8,128)(2,1)} %get-tuple-element.37.x_ref, bf16[2048,384]{1,0:T(8,128)(2,1)} %pad_maximum_fusion.1.d_ref), custom_call_target="tpu_custom_call" | custom-call | flops 3221225472 | bytes 11534336 | tf_op jit(solution)/shard_map/pallas_call | solution.py:333
  200.1 3.5 %all-to-all-done.2.d_ref = bf16[4,512,384]{2,1,0:T(8,128)(2,1)S(1)} async-done(((bf16[4,512,384]{2,1,0:T(8,128)(2,1)}), bf16[4,512,384]{2,1,0:T(8,128)(2,1)S(1)}, u32[]{:S(2)}, u32[]{:S(2)}) %all-to-all-start.2) | async-done | bytes 1572896 | tf_op jit(solution)/shard_map/all_to_all | solution.py:419
  204.7 8.7 %shard_map.109 = (f32[4,512,128]{2,1,0:T(8,128)}, f32[4,512,128]{2,1,0:T(8,128)}, f32[4,512,128]{2,1,0:T(8,128)}, f32[4,512,128]{2,1,0:T(8,128)}) custom-call(s32[16]{0:T(128)} %stack.163.ids, bf16[4,512,384]{2,1,0:T(8,128)(2,1)} %copy-done.2, bf16[4,384,2048]{2,1,0:T(8,128)(2,1)} %bitcast.75, bf16[4,384,2048]{2,1,0:T(8,128)(2,1)} %bitcast.76, ...), custom_call_target="tpu_custom_call" | custom-call | flops 3221225472 | bytes 10485760 | tf_op jit(solution)/shard_map/pallas_call | solution.py:298
  216.1 22.7 %collective-permute-done.13 = f32[4,512,128]{2,1,0:T(8,128)S(1)} collective-permute-done((f32[4,512,128]{2,1,0:T(8,128)}, f32[4,512,128]{2,1,0:T(8,128)S(1)}, u32[]{:S(2)}, u32[]{:S(2)}) %collective-permute-start.13) | collective-permute-done | bytes 1048608 | tf_op jit(solution)/shard_map/ppermute | solution.py:40
  238.7 3.6 %collective-permute-done.11 = f32[4,512,128]{2,1,0:T(8,128)S(1)} collective-permute-done((f32[4,512,128]{2,1,0:T(8,128)}, f32[4,512,128]{2,1,0:T(8,128)S(1)}, u32[]{:S(2)}, u32[]{:S(2)}) %collective-permute-start.11) | collective-permute-done | bytes 1048608 | tf_op jit(solution)/shard_map/ppermute | solution.py:40
  243.8 9.3 %all_to_all.20 = bf16[4,512,128]{2,1,0:T(8,128)(2,1)S(1)} all-to-all(bf16[4,512,128]{2,1,0:T(8,128)(2,1)S(1)} %add_convert_fusion), channel_id=1, replica_groups={{0,4,8,12},{1,5,9,13},{2,6,10,14},{3,7,11,15},{16,17,18,19},{20,21,22,2..., dimensions={0} | all-to-all | bytes 1048576 | tf_op jit(solution)/shard_map/all_to_all | solution.py:424
  253.1 17.9 %all-reduce.4.cloned.1.call-done = (f32[2048,128]{1,0:T(8,128)}, f32[2048,128]{1,0:T(8,128)}, f32[2048,128]{1,0:T(8,128)}, f32[128,2048]{1,0:T(8,128)}) async-done(((f32[2048,128]{1,0:T(8,128)}, f32[2048,128]{1,0:T(8,128)}, f32[2048,128]{1,0:T(8,128)}, f32[128,2048]{1,0:T(8,128)}), (f32[2048,128]{1,0:T(8,128)}, f32[2048,128]{1,0:T(8,128)}, f32[2048,128]{1,0:T(8,128)}, ...) | async-done | bytes 4194320 | tf_op jit(solution)/shard_map/psum | solution.py:415
  (106 shorter events, 48.2 us)
Async XLA Ops:
  7.2 128.2 %all-gather.4.cloned.1.call-start = ((), (), s32[]{:S(2)}) async-start(), calls=%async_computation.4 | async-start | bytes 8912896 | tf_op jit(solution)/shard_map/all_gather | solution.py:394
  9.1 11.5 %collective-permute-start.2 = (bf16[2048,128]{1,0:T(8,128)(2,1)}, bf16[2048,128]{1,0:T(8,128)(2,1)S(1)}, u32[]{:S(2)}, u32[]{:S(2)}) collective-permute-start(bf16[2048,128]{1,0:T(8,128)(2,1)} %param.6), channel_id=1, source_target_pairs={{0,8},{1,9},{2,10},{3,11},{4,12},{5,13},{6,14},{7,15},{8,0},{9,1},... | collective-permute-start | bytes 1572872 | tf_op jit(solution)/shard_map/ppermute | solution.py:40
  13.5 13.3 %collective-permute-start.1 = (bf16[2048,128]{1,0:T(8,128)(2,1)}, bf16[2048,128]{1,0:T(8,128)(2,1)S(1)}, u32[]{:S(2)}, u32[]{:S(2)}) collective-permute-start(bf16[2048,128]{1,0:T(8,128)(2,1)} %param.6), channel_id=1, source_target_pairs={{0,12},{1,13},{2,14},{3,15},{4,0},{5,1},{6,2},{7,3},{8,4},{9,5},{1... | collective-permute-start | bytes 1572872 | tf_op jit(solution)/shard_map/ppermute | solution.py:40
  13.9 14.0 %collective-permute-start = (bf16[2048,128]{1,0:T(8,128)(2,1)}, bf16[2048,128]{1,0:T(8,128)(2,1)S(1)}, u32[]{:S(2)}, u32[]{:S(2)}) collective-permute-start(bf16[2048,128]{1,0:T(8,128)(2,1)} %param.6), channel_id=1, source_target_pairs={{0,4},{1,5},{2,6},{3,7},{4,8},{5,9},{6,10},{7,11},{8,12},{9,13},{1... | collective-permute-start | bytes 1572872 | tf_op jit(solution)/shard_map/ppermute | solution.py:40
  29.0 21.6 %copy-start.9 = (bf16[2048,128]{1,0:T(8,128)(2,1)S(1)}, bf16[2048,128]{1,0:T(8,128)(2,1)}, u32[]{:S(2)}) copy-start(bf16[2048,128]{1,0:T(8,128)(2,1)} %param.10) | copy-start | bytes 1572868
  29.1 21.8 %copy-start.10 = (bf16[2048,128]{1,0:T(8,128)(2,1)S(1)}, bf16[2048,128]{1,0:T(8,128)(2,1)}, u32[]{:S(2)}) copy-start(bf16[2048,128]{1,0:T(8,128)(2,1)} %param.9) | copy-start | bytes 1572868
  29.1 22.8 %copy-start.11 = (bf16[2048,128]{1,0:T(8,128)(2,1)S(1)}, bf16[2048,128]{1,0:T(8,128)(2,1)}, u32[]{:S(2)}) copy-start(bf16[2048,128]{1,0:T(8,128)(2,1)} %param.8) | copy-start | bytes 1572868
  29.1 171.0 %all-gather.6.cloned.1.call-start = ((), (), s32[]{:S(2)}) async-start(), calls=%async_computation.5 | async-start | bytes 7864320 | tf_op jit(solution)/shard_map/all_gather | solution.py:400
  29.2 15.5 %collective-permute-start.3 = (bf16[2,2048,128]{2,1,0:T(8,128)(2,1)}, bf16[2,2048,128]{2,1,0:T(8,128)(2,1)}, u32[]{:S(2)}, u32[]{:S(2)}) collective-permute-start(bf16[2,2048,128]{2,1,0:T(8,128)(2,1)} %shard_map.101.refs_0_), channel_id=1, source_target_pairs={{0,1},{1,2},{2,3},{3,0},{4,5},{5,6},{6,7},{7,4},{8,9},{9,10},{10,1... | collective-permute-start | bytes 3145736 | tf_op jit(solution)/shard_map/ppermute | solution.py:40
  30.4 16.8 %collective-permute-start.6 = (bf16[2,2048,128]{2,1,0:T(8,128)(2,1)S(1)}, bf16[2,2048,128]{2,1,0:T(8,128)(2,1)}, u32[]{:S(2)}, u32[]{:S(2)}) collective-permute-start(bf16[2,2048,128]{2,1,0:T(8,128)(2,1)S(1)} %copy-done.1), channel_id=1, source_target_pairs={{0,3},{1,0},{2,1},{3,2},{4,7},{5,4},{6,5},{7,6},{8,11},{9,8},{10,9... | collective-permute-start | bytes 3145736 | tf_op jit(solution)/shard_map/ppermute | solution.py:40
  32.6 31.7 %collective-permute-start.4 = (bf16[2,2048,128]{2,1,0:T(8,128)(2,1)S(1)}, bf16[2,2048,128]{2,1,0:T(8,128)(2,1)}, u32[]{:S(2)}, u32[]{:S(2)}) collective-permute-start(bf16[2,2048,128]{2,1,0:T(8,128)(2,1)S(1)} %copy-done.1), channel_id=1, source_target_pairs={{0,1},{1,2},{2,3},{3,0},{4,5},{5,6},{6,7},{7,4},{8,9},{9,10},{10,1... | collective-permute-start | bytes 3145736 | tf_op jit(solution)/shard_map/ppermute | solution.py:40
  32.6 31.7 %collective-permute-start.5 = (bf16[2,2048,128]{2,1,0:T(8,128)(2,1)}, bf16[2,2048,128]{2,1,0:T(8,128)(2,1)}, u32[]{:S(2)}, u32[]{:S(2)}) collective-permute-start(bf16[2,2048,128]{2,1,0:T(8,128)(2,1)} %shard_map.101.refs_0_), channel_id=1, source_target_pairs={{0,3},{1,0},{2,1},{3,2},{4,7},{5,4},{6,5},{7,6},{8,11},{9,8},{10,9... | collective-permute-start | bytes 3145736 | tf_op jit(solution)/shard_map/ppermute | solution.py:40
  44.7 30.9 %collective-permute-start.7 = (bf16[2,2048,128]{2,1,0:T(8,128)(2,1)}, bf16[2,2048,128]{2,1,0:T(8,128)(2,1)}, u32[]{:S(2)}, u32[]{:S(2)}) collective-permute-start(bf16[2,2048,128]{2,1,0:T(8,128)(2,1)} %collective-permute-done.3.refs_2_), channel_id=1, source_target_pairs={{0,1},{1,2},{2,3},{3,0},{4,5},{5,6},{6,7},{7,4},{8,9},{9,10},{10,1... | collective-permute-start | bytes 3145736 | tf_op jit(solution)/shard_map/ppermute | solution.py:40
  47.2 34.4 %collective-permute-start.8 = (bf16[2,2048,128]{2,1,0:T(8,128)(2,1)}, bf16[2,2048,128]{2,1,0:T(8,128)(2,1)}, u32[]{:S(2)}, u32[]{:S(2)}) collective-permute-start(bf16[2,2048,128]{2,1,0:T(8,128)(2,1)} %collective-permute-done.6.refs_5_), channel_id=1, source_target_pairs={{0,3},{1,0},{2,1},{3,2},{4,7},{5,4},{6,5},{7,6},{8,11},{9,8},{10,9... | collective-permute-start | bytes 3145736 | tf_op jit(solution)/shard_map/ppermute | solution.py:40
  94.1 17.6 %copy-start.14 = (f32[128,256]{1,0:T(8,128)S(1)}, f32[128,256]{1,0:T(8,128)}, u32[]{:S(2)}) copy-start(f32[128,256]{1,0:T(8,128)} %get-tuple-element.25) | copy-start | bytes 393220
  99.9 18.2 %all-to-all-start = ((bf16[8,64,256]{2,1,0:T(8,128)(2,1)}), bf16[8,64,256]{2,1,0:T(8,128)(2,1)S(1)}, u32[]{:S(2)}, u32[]{:S(2)}) async-start(bf16[8,64,256]{2,1,0:T(8,128)(2,1)} %bitcast_dynamic-update-slice_fusion), calls=%async_computation | async-start | bytes 524288 | tf_op jit(solution)/shard_map/all_to_all | solution.py:362
  111.7 6.5 %collective-permute-start.9 = (bf16[128,256]{1,0:T(8,128)(2,1)S(1)}, bf16[128,256]{1,0:T(8,128)(2,1)S(1)}, u32[]{:S(2)}, u32[]{:S(2)}) collective-permute-start(bf16[128,256]{1,0:T(8,128)(2,1)S(1)} %convert_element_type.15), channel_id=1, source_target_pairs={{0,16},{16,0},{32,48},{48,32},{64,80},{80,64},{96,112},{112,96},{1... | collective-permute-start | bytes 196616 | tf_op jit(solution)/shard_map/ppermute | solution.py:57
  167.6 13.9 %all-to-all-start.1 = ((f32[8,64,256]{2,1,0:T(8,128)}), f32[8,64,256]{2,1,0:T(8,128)S(1)}, u32[]{:S(2)}, u32[]{:S(2)}) async-start(f32[8,64,256]{2,1,0:T(8,128)} %pad_dynamic-update-slice_fusion), calls=%async_computation.1 | async-start | bytes 1048576 | tf_op jit(solution)/shard_map/all_to_all | solution.py:379
  172.0 5.8 %collective-permute-start.10 = (f32[128,256]{1,0:T(8,128)S(1)}, f32[128,256]{1,0:T(8,128)S(1)}, u32[]{:S(2)}, u32[]{:S(2)}) collective-permute-start(f32[128,256]{1,0:T(8,128)S(1)} %get-tuple-element.49), channel_id=1, source_target_pairs={{0,16},{16,0},{32,48},{48,32},{64,80},{80,64},{96,112},{112,96},{1... | collective-permute-start | bytes 393224 | tf_op jit(solution)/shard_map/ppermute | solution.py:57
  186.0 17.5 %all-to-all-start.2 = ((bf16[4,512,384]{2,1,0:T(8,128)(2,1)}), bf16[4,512,384]{2,1,0:T(8,128)(2,1)S(1)}, u32[]{:S(2)}, u32[]{:S(2)}) async-start(bf16[4,512,384]{2,1,0:T(8,128)(2,1)} %bitcast.51), calls=%async_computation.2 | async-start | bytes 3145728 | tf_op jit(solution)/shard_map/all_to_all | solution.py:419
  190.7 80.4 %all-reduce.4.cloned.1.call-start = ((), (), s32[]{:S(2)}) async-start(), calls=%async_computation.6 | async-start | bytes 8388608 | tf_op jit(solution)/shard_map/psum | solution.py:415
  213.4 25.3 %collective-permute-start.13 = (f32[4,512,128]{2,1,0:T(8,128)}, f32[4,512,128]{2,1,0:T(8,128)S(1)}, u32[]{:S(2)}, u32[]{:S(2)}) collective-permute-start(f32[4,512,128]{2,1,0:T(8,128)} %get-tuple-element.36), channel_id=1, source_target_pairs={{0,3},{1,0},{2,1},{3,2},{4,7},{5,4},{6,5},{7,6},{8,11},{9,8},{10,9... | collective-permute-start | bytes 3145736 | tf_op jit(solution)/shard_map/ppermute | solution.py:40
  215.4 23.3 %collective-permute-start.12 = (f32[4,512,128]{2,1,0:T(8,128)}, f32[4,512,128]{2,1,0:T(8,128)S(1)}, u32[]{:S(2)}, u32[]{:S(2)}) collective-permute-start(f32[4,512,128]{2,1,0:T(8,128)} %get-tuple-element.35), channel_id=1, source_target_pairs={{0,2},{1,3},{2,0},{3,1},{4,6},{5,7},{6,4},{7,5},{8,10},{9,11},{10,... | collective-permute-start | bytes 3145736 | tf_op jit(solution)/shard_map/ppermute | solution.py:40
  215.8 26.5 %collective-permute-start.11 = (f32[4,512,128]{2,1,0:T(8,128)}, f32[4,512,128]{2,1,0:T(8,128)S(1)}, u32[]{:S(2)}, u32[]{:S(2)}) collective-permute-start(f32[4,512,128]{2,1,0:T(8,128)} %get-tuple-element.34), channel_id=1, source_target_pairs={{0,1},{1,2},{2,3},{3,0},{4,5},{5,6},{6,7},{7,4},{8,9},{9,10},{10,1... | collective-permute-start | bytes 3145736 | tf_op jit(solution)/shard_map/ppermute | solution.py:40
  (13 other events, 33.3 us)
Sparse Core Ops, SparseCore 0:
  29.2 87.9 all-gather.3
  118.9 42.1 all-gather.5
  199.5 71.5 all-reduce.3

commit v2 on v1

v2 whole, which is shorter than its diff:
```python
import functools
import math

import jax
import jax.numpy as jnp
from jax import lax
from jax.experimental import pallas as pl
from jax.experimental.pallas import tpu as pltpu
from jax.sharding import PartitionSpec as P

DH = 128
RATIO = 16
NX = 4
NZ = 4
NY = 4
BF = jnp.bfloat16
F32 = jnp.float32
STEPS = (0, 1, -1, 2)
LOG2E = 1.0 / math.log(2.0)
NT = (((1,), (1,)), ((), ()))
NN = (((1,), (0,)), ((), ()))


def mm(a, b, dims=NN):
    return lax.dot_general(a, b, dims, preferred_element_type=F32)


def place(ctx, first, second):
    x, z = (first, second) if ctx % 2 == 0 else (second, first)
    return ctx * NX * NZ + x * NZ + z


def send(value, first, second):
    pairs = [
        (place(ctx, a, b), place(ctx, (a + first) % NX, (b + second) % NZ))
        for ctx in range(NY * 2)
        for a in range(NX)
        for b in range(NZ)
    ]
    return lax.ppermute(value, ("ctx", "tp"), pairs)


def first_lines():
    return [
        [place(ctx, a, b) for a in range(NX)] for ctx in range(NY * 2) for b in range(NZ)
    ]


def position():
    me = lax.axis_index("tp")
    x, z = me // NZ, me % NZ
    even = lax.axis_index("ctx") % 2 == 0
    return even, jnp.where(even, x, z), jnp.where(even, z, x)


def send_core(value):
    return lax.ppermute(value, "ctx", [(i, i ^ 1) for i in range(NY * 2)])


def order_kernel(x_ref, dep_ref, out_ref):
    pass


def after(value, dep):
    return pl.pallas_call(
        order_kernel,
        in_specs=[pl.BlockSpec(memory_space=pl.ANY)] * 2,
        out_specs=pl.BlockSpec(memory_space=pl.ANY),
        out_shape=jax.ShapeDtypeStruct(value.shape, value.dtype),
        input_output_aliases={0: 0},
    )(value, dep)


def gather_features(block):
    up, down, far = [send(block, step, 0) for step in STEPS[1:]]
    near, rest = jnp.stack([block, up]), jnp.stack([down, far])
    near, rest = after(near, rest), after(rest, near)
    near_up, rest_down = send(near, 0, 1), send(rest, 0, -1)
    near_down, rest_up = send(near, 0, -1), send(rest, 0, 1)
    near_far, rest_far = send(near_up, 0, 1), send(rest_down, 0, -1)
    return [near, rest, near_up, rest_up, near_down, rest_down, near_far, rest_far]


def block_ids():
    even, first, second = position()
    ids = []
    for b in STEPS:
        for a in STEPS:
            i, j = (first - a) % NX, (second - b) % NZ
            ids.append(jnp.where(even, i * NZ + j, j * NZ + i))
    return jnp.stack(ids).astype(jnp.int32)


def sibling_ids():
    me = lax.axis_index("ctx")
    return jnp.stack([((me >> 1) ^ 1) * 2, ((me >> 2) ^ 1) * 4]).astype(jnp.int32)


def project_kernel(ids, sibs, *refs):
    parts = refs[:8]
    w_ref, full_ref, q_ref, kv_ref, first_ref, others_ref, second_ref, last_ref = refs[8:]
    step = pl.program_id(0)
    for i in range(16):
        start = pl.multiple_of(ids[i] * 128, 128)
        full_ref[:, pl.ds(start, 128)] = parts[i // 2][i % 2]
    out = mm(full_ref[...], w_ref[...]).astype(BF)
    q_ref[...] = out[:, :DH]
    kv = out[:, DH:]
    kv_ref[...] = kv
    rows = kv.shape[0]
    for l, ref in enumerate((first_ref, second_ref, last_ref)):
        width = RATIO * 2**l
        count = rows // width
        window = lax.broadcasted_iota(jnp.int32, (count, rows), 0)
        row = lax.broadcasted_iota(jnp.int32, (count, rows), 1)
        inside = jnp.where((row >= window * width) & (row < (window + 1) * width), 1.0, 0.0)
        means = mm(inside.astype(BF), kv) * (1.0 / width)
        if l == 0:
            ref[...] = means.astype(BF)
        else:
            ref[pl.ds(pl.multiple_of(step * count, count), count), :] = means

    @pl.when(step == pl.num_programs(0) - 1)
    def _():
        second = second_ref[...].astype(BF)
        last = last_ref[...].astype(BF)
        for d in range(NY * 2):
            others_ref[d] = second
        for d in range(4):
            others_ref[pl.ds(sibs[1] + d, 1), : last.shape[0]] = last[None]


def project(ids, sibs, parts, weight):
    n = parts[0].shape[1]
    feats = 16 * 128
    rows = 512
    row_map = lambda i, ids, sibs: (i, 0)
    coarse = n // RATIO
    return pl.pallas_call(
        project_kernel,
        grid_spec=pltpu.PrefetchScalarGridSpec(
            num_scalar_prefetch=2,
            grid=(n // rows,),
            in_specs=[pl.BlockSpec((2, rows, 128), lambda i, ids, sibs: (0, i, 0))] * 8
            + [pl.BlockSpec(weight.shape, lambda i, ids, sibs: (0, 0))],
            out_specs=[
                pl.BlockSpec((rows, feats), row_map),
                pl.BlockSpec((rows, DH), row_map),
                pl.BlockSpec((rows, 2 * DH), row_map),
                pl.BlockSpec((rows // RATIO, 2 * DH), row_map),
                pl.BlockSpec((NY * 2, coarse // 2, 2 * DH), lambda i, ids, sibs: (0, 0, 0)),
            ],
            scratch_shapes=[
                pltpu.VMEM((coarse // 2, 2 * DH), F32),
                pltpu.VMEM((coarse // 4, 2 * DH), F32),
            ],
        ),
        out_shape=[
            jax.ShapeDtypeStruct((n, feats), BF),
            jax.ShapeDtypeStruct((n, DH), BF),
            jax.ShapeDtypeStruct((n, 2 * DH), BF),
            jax.ShapeDtypeStruct((coarse, 2 * DH), BF),
            jax.ShapeDtypeStruct((NY * 2, coarse // 2, 2 * DH), BF),
        ],
        compiler_params=pltpu.CompilerParams(vmem_limit_bytes=60 * 2**20),
        cost_estimate=pl.CostEstimate(
            flops=6 * n * feats * DH, bytes_accessed=4 * n * feats, transcendentals=0
        ),
    )(ids, sibs, *parts, weight)


def add_bias(scores, own, coarse):
    out = [scores[:own]]
    for l in range((scores.shape[0] - own) // coarse):
        low = own + l * coarse
        out.append(scores[low : low + coarse] + math.log(RATIO * 2**l) * LOG2E)
    return jnp.concatenate(out, axis=0)


def attention_kernel(
    own, coarse, sibs, q_ref, kv_ref, first_ref, others_ref, cot_ref, wo_ref,
    att_ref, dq_ref, dkv_ref, dfirst_ref, dothers_ref, k_ref, v_ref, kt_ref, vt_ref, acc_ref,
):
    step = pl.program_id(0)

    @pl.when(step == 0)
    def _():
        half, quarter = coarse // 2, coarse // 4
        pieces = [(0, kv_ref[...]), (own, first_ref[...])]
        for d in range(2):
            pieces.append((own + coarse + d * half, others_ref[pl.ds(sibs[0] + d, 1)][0]))
        for d in range(4):
            rows = others_ref[pl.ds(sibs[1] + d, 1)][0, :quarter]
            pieces.append((own + 2 * coarse + d * quarter, rows))
        for low, rows in pieces:
            k_ref[low : low + rows.shape[0]] = rows[:, :DH]
            v_ref[low : low + rows.shape[0]] = rows[:, DH:]
        kt_ref[...] = k_ref[...].T
        vt_ref[...] = v_ref[...].T
        acc_ref[...] = jnp.zeros_like(acc_ref)

    q = q_ref[...]
    d_att = mm(cot_ref[...], wo_ref[...], NT).astype(BF)
    scores = mm(k_ref[...], q, NT) * (DH**-0.5 * LOG2E)
    scores = add_bias(scores, own, coarse)
    d_probs = mm(v_ref[...], d_att, NT)
    peak = jnp.max(scores, axis=0, keepdims=True)
    expo = jnp.exp2(scores - peak)
    probs = expo * (1.0 / jnp.sum(expo, axis=0, keepdims=True))
    delta = jnp.sum(probs * d_probs, axis=0, keepdims=True)
    d_scores = (DH**-0.5 * probs * (d_probs - delta)).astype(BF)
    probs = probs.astype(BF)
    att_ref[...] = mm(vt_ref[...], probs).astype(BF)
    dq_ref[...] = mm(kt_ref[...], d_scores).T.astype(BF)
    acc_ref[:, :DH] += mm(d_scores, q)
    acc_ref[:, DH:] += mm(probs, d_att)

    @pl.when(step == pl.num_programs(0) - 1)
    def _():
        half, quarter = coarse // 2, coarse // 4
        dkv_ref[...] = acc_ref[:own]
        dfirst_ref[...] = acc_ref[own : own + coarse]
        dothers_ref[...] = jnp.zeros_like(dothers_ref)
        for d in range(2):
            low = own + coarse + d * half
            dothers_ref[pl.ds(sibs[0] + d, 1)] = acc_ref[low : low + half][None]
        for d in range(4):
            low = own + 2 * coarse + d * quarter
            dothers_ref[pl.ds(sibs[1] + d, 1), :quarter] = acc_ref[low : low + quarter][None]


def attention(sibs, queries, listed, first, others, cot, w_out):
    n, feats = cot.shape
    own, coarse = listed.shape[0], first.shape[0]
    m = own + 3 * coarse
    rows = 512
    whole = lambda i, sibs: (0, 0)
    blocks = lambda i, sibs: (0, 0, 0)
    return pl.pallas_call(
        functools.partial(attention_kernel, own, coarse),
        grid_spec=pltpu.PrefetchScalarGridSpec(
            num_scalar_prefetch=1,
            grid=(n // rows,),
            in_specs=[
                pl.BlockSpec((rows, DH), lambda i, sibs: (i, 0)),
                pl.BlockSpec(listed.shape, whole),
                pl.BlockSpec(first.shape, whole),
                pl.BlockSpec(others.shape, blocks),
                pl.BlockSpec((rows, feats), lambda i, sibs: (i, 0)),
                pl.BlockSpec((DH, feats), whole),
            ],
            out_specs=[
                pl.BlockSpec((DH, rows), lambda i, sibs: (0, i)),
                pl.BlockSpec((rows, DH), lambda i, sibs: (i, 0)),
                pl.BlockSpec(listed.shape, whole),
                pl.BlockSpec(first.shape, whole),
                pl.BlockSpec(others.shape, blocks),
            ],
            scratch_shapes=[
                pltpu.VMEM((m, DH), BF),
                pltpu.VMEM((m, DH), BF),
                pltpu.VMEM((DH, m), BF),
                pltpu.VMEM((DH, m), BF),
                pltpu.VMEM((m, 2 * DH), F32),
            ],
        ),
        out_shape=[
            jax.ShapeDtypeStruct((DH, n), BF),
            jax.ShapeDtypeStruct((n, DH), BF),
            jax.ShapeDtypeStruct(listed.shape, F32),
            jax.ShapeDtypeStruct(first.shape, F32),
            jax.ShapeDtypeStruct(others.shape, F32),
        ],
        compiler_params=pltpu.CompilerParams(vmem_limit_bytes=60 * 2**20),
        cost_estimate=pl.CostEstimate(
            flops=24 * n * m * DH, bytes_accessed=2 * n * feats, transcendentals=n * m
        ),
    )(sibs, queries, listed, first, others, cot, w_out)


def token_grad_kernel(ids, d_ref, *refs):
    weights, outs = refs[:NZ], refs[NZ:]
    d = jnp.concatenate([d_ref[i] for i in range(NX)], axis=1)
    w = jnp.concatenate(
        [jnp.concatenate([w_ref[i] for w_ref in weights], axis=0) for i in range(NX)], axis=1
    )
    out = mm(d, w, NT)
    for step, out_ref in enumerate(outs):
        out_ref[0] = out[:, step * DH : (step + 1) * DH]


def token_grad_parts(d_rows, weights):
    heads, rows, cols = d_rows.shape
    even, _, second = position()
    ids = []
    for i in range(NX):
        for step in range(NZ):
            j = (second + step) % NZ
            ids.append(jnp.where(even, i * NZ + j, j * NZ + i))
    ids = jnp.stack(ids).astype(jnp.int32)

    def column(step):
        return pl.BlockSpec((heads, DH, cols), lambda i, ids: (0, ids[i * NZ + step], 0))

    return pl.pallas_call(
        token_grad_kernel,
        grid_spec=pltpu.PrefetchScalarGridSpec(
            num_scalar_prefetch=1,
            grid=(NX,),
            in_specs=[pl.BlockSpec((heads, rows, cols), lambda i, ids: (0, 0, 0))]
            + [column(step) for step in range(NZ)],
            out_specs=[pl.BlockSpec((1, rows, DH), lambda i, ids: (i, 0, 0))] * NZ,
        ),
        out_shape=[jax.ShapeDtypeStruct((NX, rows, DH), F32)] * NZ,
        compiler_params=pltpu.CompilerParams(vmem_limit_bytes=60 * 2**20),
        cost_estimate=pl.CostEstimate(
            flops=2 * heads * rows * cols * 2048,
            bytes_accessed=2 * heads * cols * 2048 + 8192 * rows,
            transcendentals=0,
        ),
    )(ids, d_rows, weights, weights, weights, weights)


def chunk_ids():
    c = lax.axis_index("ctx") % 2
    return jnp.stack([j * 2 + core for core in (1 - c, c) for j in range(NY)]).astype(jnp.int32)


def out_grad_kernel(chunks, x_ref, a_ref, give_ref, keep_ref):
    step = pl.program_id(0)
    grads = mm(a_ref[...], x_ref[...]).T

    @pl.when(step < NY)
    def _():
        give_ref[0, 0] = grads

    @pl.when(step >= NY)
    def _():
        keep_ref[0, 0] = grads


def out_grads(chunks, cot, attended_t):
    n, f = cot.shape
    cols = f // (2 * NY)
    shape = jax.ShapeDtypeStruct((NY, 4, cols, DH), F32)
    return pl.pallas_call(
        out_grad_kernel,
        grid_spec=pltpu.PrefetchScalarGridSpec(
            num_scalar_prefetch=1,
            grid=(2 * NY,),
            in_specs=[
                pl.BlockSpec((n, cols), lambda i, chunks: (0, chunks[i])),
                pl.BlockSpec((DH, n), lambda i, chunks: (0, 0)),
            ],
            out_specs=[
                pl.BlockSpec(
                    (1, 1, cols, DH), lambda i, chunks: (jnp.minimum(i, NY - 1), 3, 0, 0)
                ),
                pl.BlockSpec(
                    (1, 1, cols, DH), lambda i, chunks: (jnp.maximum(i - NY, 0), 3, 0, 0)
                ),
            ],
        ),
        out_shape=[shape, shape],
        compiler_params=pltpu.CompilerParams(vmem_limit_bytes=60 * 2**20),
        cost_estimate=pl.CostEstimate(
            flops=2 * n * f * DH, bytes_accessed=2 * n * f, transcendentals=0
        ),
    )(chunks, cot, attended_t)


def store_grads(out_ref, d_t, x):
    grads = mm(d_t, x).T
    for i in range(3):
        out_ref[0, i] = grads[:, i * DH : (i + 1) * DH]


def give_kernel(
    chunks, sibs, x_ref, dq_ref, own_ref, first_ref, others_ref, alias_ref, out_ref, d_ref, dt_ref
):
    @pl.when(pl.program_id(0) == 0)
    def _():
        coarse, cols = first_ref.shape
        half, quarter = coarse // 2, coarse // 4
        second = sum(others_ref[pl.ds(sibs[0] + d, 1)][0] for d in range(2))
        last = sum(others_ref[pl.ds(sibs[1] + d, 1)][0, :quarter] for d in range(4))
        total = own_ref[...]
        for l, grads in enumerate((first_ref[...], second, last)):
            width = RATIO * 2**l
            spread = jnp.broadcast_to(
                (grads * (1.0 / width))[:, None, :], (grads.shape[0], width, cols)
            )
            total = total + spread.reshape(total.shape)
        d_ref[:, :DH] = dq_ref[...]
        d_ref[:, DH:] = total.astype(BF)
        dt_ref[...] = d_ref[...].T

    store_grads(out_ref, dt_ref[...], x_ref[...])


def keep_kernel(chunks, x_ref, dt_ref, alias_ref, out_ref):
    store_grads(out_ref, dt_ref[...], x_ref[...])


def weight_grads_give(chunks, sibs, feats, d_queries, own, first, others, give):
    n, f = feats.shape
    cols = f // (2 * NY)
    whole = lambda i, chunks, sibs: (0, 0)
    return pl.pallas_call(
        give_kernel,
        grid_spec=pltpu.PrefetchScalarGridSpec(
            num_scalar_prefetch=2,
            grid=(NY,),
            in_specs=[
                pl.BlockSpec((n, cols), lambda i, chunks, sibs: (0, chunks[i])),
                pl.BlockSpec(d_queries.shape, whole),
                pl.BlockSpec(own.shape, whole),
                pl.BlockSpec(first.shape, whole),
                pl.BlockSpec(others.shape, lambda i, chunks, sibs: (0, 0, 0)),
                pl.BlockSpec(memory_space=pl.ANY),
            ],
            out_specs=[
                pl.BlockSpec((1, 3, cols, DH), lambda i, chunks, sibs: (i, 0, 0, 0)),
                pl.BlockSpec((n, 3 * DH), whole),
                pl.BlockSpec((3 * DH, n), whole),
            ],
        ),
        out_shape=[
            jax.ShapeDtypeStruct(give.shape, F32),
            jax.ShapeDtypeStruct((n, 3 * DH), BF),
            jax.ShapeDtypeStruct((3 * DH, n), BF),
        ],
        input_output_aliases={7: 0},
        compiler_params=pltpu.CompilerParams(vmem_limit_bytes=60 * 2**20),
        cost_estimate=pl.CostEstimate(
            flops=3 * n * f * DH, bytes_accessed=n * f + 6 * f * DH, transcendentals=0
        ),
    )(chunks, sibs, feats, d_queries, own, first, others, give)


def weight_grads_keep(chunks, feats, d_t, keep):
    n, f = feats.shape
    cols = f // (2 * NY)
    return pl.pallas_call(
        keep_kernel,
        grid_spec=pltpu.PrefetchScalarGridSpec(
            num_scalar_prefetch=1,
            grid=(NY,),
            in_specs=[
                pl.BlockSpec((n, cols), lambda i, chunks: (0, chunks[NY + i])),
                pl.BlockSpec(d_t.shape, lambda i, chunks: (0, 0)),
                pl.BlockSpec(memory_space=pl.ANY),
            ],
            out_specs=pl.BlockSpec((1, 3, cols, DH), lambda i, chunks: (i, 0, 0, 0)),
        ),
        out_shape=jax.ShapeDtypeStruct(keep.shape, F32),
        input_output_aliases={3: 0},
        compiler_params=pltpu.CompilerParams(vmem_limit_bytes=60 * 2**20),
        cost_estimate=pl.CostEstimate(
            flops=3 * n * f * DH, bytes_accessed=n * f + 6 * f * DH, transcendentals=0
        ),
    )(chunks, feats, d_t, keep)


def sum_ctx(give, keep, dep):
    halves = keep + send_core(give)
    columns = [[y * 2 + c for y in range(NY)] for c in range(2)]
    total = lax.psum_scatter(halves, "ctx", scatter_dimension=0, axis_index_groups=columns)
    grads = lax.all_gather(after(total, dep), "ctx")
    rows = grads.shape[0] * grads.shape[2]
    return [grads[:, i].reshape(rows, DH) for i in range(4)]


def body(tokens, cotangent, w_query, w_key, w_value, w_out):
    own = tokens.shape[0]
    ids, sibs, lines = block_ids(), sibling_ids(), first_lines()
    weights = jnp.concatenate([w_query, w_key, w_value], axis=1)
    tok_parts = gather_features(tokens)
    cot = lax.all_gather(after(cotangent, tok_parts[1]), "tp", axis=1, tiled=True)
    feats, queries, keys_values, first, others = project(ids, sibs, tok_parts, weights)
    others = lax.all_to_all(others, "ctx", 0, 0)
    first = send_core(first)
    weight_heads = lax.all_gather(
        after(weights, queries), ("ctx", "tp"), axis_index_groups=lines
    )
    attended_t, d_queries, d_own, d_first, d_others = attention(
        sibs, queries, keys_values, first, others, cot, w_out
    )
    chunks = chunk_ids()
    give, keep = out_grads(chunks, cot, attended_t)
    d_others = lax.all_to_all(d_others, "ctx", 0, 0)
    d_first = send_core(d_first)
    give, d_all, d_t = weight_grads_give(
        chunks, sibs, feats, d_queries, d_own, d_first, d_others, give
    )
    keep = weight_grads_keep(chunks, feats, d_t, keep)
    d_rows = d_all.reshape(NX, own // NX, 3 * DH)
    d_rows = lax.all_to_all(d_rows, ("ctx", "tp"), 0, 0, axis_index_groups=lines)
    parts = token_grad_parts(d_rows, weight_heads)
    query_grad, key_grad, value_grad, out_grad = sum_ctx(give, keep, parts[0])
    out_grad = out_grad.T
    total = parts[0]
    for step in range(1, NZ):
        total = total + send(parts[step], 0, step)
    token_grad = lax.all_to_all(
        total.astype(BF), ("ctx", "tp"), 0, 0, axis_index_groups=lines
    ).reshape(own, DH)
    return (token_grad, query_grad, key_grad, value_grad, out_grad)


def solution(mesh):
    return jax.shard_map(
        body,
        mesh=mesh,
        in_specs=(
            P("ctx", "tp"),
            P("ctx", "tp"),
            P(None, "tp"),
            P(None, "tp"),
            P(None, "tp"),
            P("tp", None),
        ),
        out_specs=(P("ctx", "tp"), P(None, "tp"), P(None, "tp"), P(None, "tp"), P("tp", None)),
        check_vma=False,
    )
```

time: 285 us -> 266 us (0.933)
  other arithmetic: 14.7 us -> 5.21 us
  matrix products: 5.61 us -> 0 us
  local copies, waits for them, and re-layouts: 20.1 us -> 15.7 us
  waiting for transfers between devices: 104 us -> 101 us
    psum x1 -> x0, waiting for transfers between devices: 17.9 us -> none  [body(): lax.psum(tuple(weight_grads(feats, d_all)) + (out_part,), 'ctx')]
    all_to_all x1, waiting for transfers between devices: 3.46 us -> 12 us  [body(): lax.all_to_all(d_rows, ('ctx', 'tp'), 0, 0, axis_index_groups=lines)]
    unnamed x44 -> x31, local copies, waits for them, and re-layouts: 14 us -> 7.36 us
    dot_general x1 -> x0, matrix products: 5.61 us -> none  [mm(): return lax.dot_general(a, b, dims, preferred_element_type=F32)]
    all_to_all x2, waiting for transfers between devices: 9.9 us -> 5.29 us  [the longest x1 5.29 us: body(): others = lax.all_to_all(others, 'ctx', 0, 0)]
    unnamed x7 -> x0, other arithmetic: 4.36 us -> none
    all_gather x1, waiting for transfers between devices: 0.01 us -> 4.1 us  [body(): lax.all_gather(after(cotangent, tok_parts[1]), 'tp', axis=1, tiled=True)]
    add x0 -> x1, other arithmetic: none -> 3.18 us  [sum_ctx(): halves = keep + send_core(give)]
  transfers between devices with their start and end apart: 20 -> 22, of which waited for: 13 -> 14; matrix products, arithmetic and copies ran while one was open for 10% -> 4% of each run, Pallas kernels for 27% -> 28%
where the time goes in v2:
time: 266 us; the launch traced here: 263 us
  waiting for transfers between devices  101 us (38%)
  Pallas kernels  73 us (27%)
  starting transfers between devices  43.2 us (16%)
  local copies, waits for them, and re-layouts  15.7 us (6%)
  between operations  13.9 us (5%)
  blocking collectives  10.9 us (4%)
  other arithmetic  5.21 us (2%)
    ppermute x12, waiting for transfers between devices, send(): return lax.ppermute(value, ('ctx', 'tp'), pairs)  75.8 us
    pallas_call x1, Pallas kernels, attention(): pl.pallas_call(functools.partial(attention_kernel, own, coarse), grid_spe...  27.7 us
    ppermute x12, starting transfers between devices, send(): return lax.ppermute(value, ('ctx', 'tp'), pairs)  20.1 us
    pallas_call x1, Pallas kernels, project(): pl.pallas_call(project_kernel, grid_spec=pltpu.PrefetchScalarGridSpec(num...  13.1 us
    all_to_all x1, waiting for transfers between devices, body(): lax.all_to_all(d_rows, ('ctx', 'tp'), 0, 0, axis_index_groups=lines)  12 us
    all_to_all x1, starting transfers between devices, body(): others = lax.all_to_all(others, 'ctx', 0, 0)  11.8 us
    all_to_all x1, blocking collectives, body(): lax.all_to_all(total.astype(BF), ('ctx', 'tp'), 0, 0, axis_index_groups=l...  10.9 us
    pallas_call x1, Pallas kernels, out_grads(): pl.pallas_call(out_grad_kernel, grid_spec=pltpu.PrefetchScalarGridSpec(nu...  9.02 us
  transfers between devices with their start and end apart: 22, of which 14 were waited for; matrix products, arithmetic and copies ran while one was open for 4% of the time, Pallas kernels for 28%

profile of v2, /device:TPU:1, one launch (start us, length us, event | category | flops | bytes accessed | tf_op | source)
XLA Modules:
  0.0 263.2 jit_solution(6620210296612827978)
XLA Ops:
  9.1 4.4 %collective-permute-start.2 = (bf16[2048,128]{1,0:T(8,128)(2,1)}, bf16[2048,128]{1,0:T(8,128)(2,1)S(1)}, u32[]{:S(2)}, u32[]{:S(2)}) collective-permute-start(bf16[2048,128]{1,0:T(8,128)(2,1)} %param.6), channel_id=1, source_target_pairs={{0,8},{1,9},{2,10},{3,11},{4,12},{5,13},{6,14},{7,15},{8,0},{9,1},... | collective-permute-start | bytes 1572872 | tf_op jit(solution)/shard_map/ppermute | solution.py:40
  15.0 5.6 %collective-permute-done.2 = bf16[2048,128]{1,0:T(8,128)(2,1)S(1)} collective-permute-done((bf16[2048,128]{1,0:T(8,128)(2,1)}, bf16[2048,128]{1,0:T(8,128)(2,1)S(1)}, u32[]{:S(2)}, u32[]{:S(2)}) %collective-permute-start.2) | collective-permute-done | bytes 524320 | tf_op jit(solution)/shard_map/ppermute | solution.py:40
  20.6 6.2 %collective-permute-done.1 = bf16[2048,128]{1,0:T(8,128)(2,1)S(1)} collective-permute-done((bf16[2048,128]{1,0:T(8,128)(2,1)}, bf16[2048,128]{1,0:T(8,128)(2,1)S(1)}, u32[]{:S(2)}, u32[]{:S(2)}) %collective-permute-start.1) | collective-permute-done | bytes 524320 | tf_op jit(solution)/shard_map/ppermute | solution.py:40
  35.7 9.4 %collective-permute-done.3.refs_2_ = bf16[2,2048,128]{2,1,0:T(8,128)(2,1)} collective-permute-done((bf16[2,2048,128]{2,1,0:T(8,128)(2,1)}, bf16[2,2048,128]{2,1,0:T(8,128)(2,1)}, u32[]{:S(2)}, u32[]{:S(2)}) %collective-permute-start.3) | collective-permute-done | bytes 1048608 | tf_op jit(solution)/shard_map/ppermute | solution.py:40
  47.6 3.5 %collective-permute-start.8 = (bf16[2,2048,128]{2,1,0:T(8,128)(2,1)}, bf16[2,2048,128]{2,1,0:T(8,128)(2,1)}, u32[]{:S(2)}, u32[]{:S(2)}) collective-permute-start(bf16[2,2048,128]{2,1,0:T(8,128)(2,1)} %collective-permute-done.6.refs_5_), channel_id=1, source_target_pairs={{0,3},{1,0},{2,1},{3,2},{4,7},{5,4},{6,5},{7,6},{8,11},{9,8},{10,9... | collective-permute-start | bytes 3145736 | tf_op jit(solution)/shard_map/ppermute | solution.py:40
  54.9 9.9 %collective-permute-done.4.refs_3_ = bf16[2,2048,128]{2,1,0:T(8,128)(2,1)} collective-permute-done((bf16[2,2048,128]{2,1,0:T(8,128)(2,1)S(1)}, bf16[2,2048,128]{2,1,0:T(8,128)(2,1)}, u32[]{:S(2)}, u32[]{:S(2)}) %collective-permute-start.4) | collective-permute-done | bytes 1048608 | tf_op jit(solution)/shard_map/ppermute | solution.py:40
  64.8 11.2 %collective-permute-done.7.refs_6_ = bf16[2,2048,128]{2,1,0:T(8,128)(2,1)} collective-permute-done((bf16[2,2048,128]{2,1,0:T(8,128)(2,1)}, bf16[2,2048,128]{2,1,0:T(8,128)(2,1)}, u32[]{:S(2)}, u32[]{:S(2)}) %collective-permute-start.7) | collective-permute-done | bytes 1048608 | tf_op jit(solution)/shard_map/ppermute | solution.py:40
  76.0 6.0 %collective-permute-done.8.refs_7_ = bf16[2,2048,128]{2,1,0:T(8,128)(2,1)} collective-permute-done((bf16[2,2048,128]{2,1,0:T(8,128)(2,1)}, bf16[2,2048,128]{2,1,0:T(8,128)(2,1)}, u32[]{:S(2)}, u32[]{:S(2)}) %collective-permute-start.8) | collective-permute-done | bytes 1048608 | tf_op jit(solution)/shard_map/ppermute | solution.py:40
  82.0 13.1 %shard_map.103 = (bf16[2048,2048]{1,0:T(8,128)(2,1)}, bf16[2048,128]{1,0:T(8,128)(2,1)}, bf16[2048,256]{1,0:T(8,128)(2,1)}, bf16[128,256]{1,0:T(8,128)(2,1)}, bf16[8,64,256]{2,1,0:T(8,128)(2,1)}) custom-call(s32[16]{0:T(128)} %stack.201.ids, s32[2]{0:T(128)} %pad_add_fusion.sibs, bf16[2,2048,128]{2,1,0:T(8,128)(2,1)} %shard_map.101.refs_0_, ...), custom_call_target="tpu_custom_call" | custom-call | flops 3221225472 | bytes 16777216 | tf_op jit(solution)/shard_map/pallas_call | solution.py:139
  95.2 11.8 %all-to-all-start = ((bf16[8,64,256]{2,1,0:T(8,128)(2,1)}), bf16[8,64,256]{2,1,0:T(8,128)(2,1)S(1)}, u32[]{:S(2)}, u32[]{:S(2)}) async-start(bf16[8,64,256]{2,1,0:T(8,128)(2,1)} %get-tuple-element.28), calls=%async_computation | async-start | bytes 524288 | tf_op jit(solution)/shard_map/all_to_all | solution.py:481
  108.2 5.3 %all-to-all-done.others_ref = bf16[8,64,256]{2,1,0:T(8,128)(2,1)S(1)} async-done(((bf16[8,64,256]{2,1,0:T(8,128)(2,1)}), bf16[8,64,256]{2,1,0:T(8,128)(2,1)S(1)}, u32[]{:S(2)}, u32[]{:S(2)}) %all-to-all-start) | async-done | bytes 262176 | tf_op jit(solution)/shard_map/all_to_all | solution.py:481
  113.5 4.1 %all-gather.6.cloned.1.call-done.cot_ref.x_ref = bf16[2048,2048]{1,0:T(8,128)(2,1)} async-done(((bf16[2048,128]{1,0:T(8,128)(2,1)}), bf16[2048,2048]{1,0:T(8,128)(2,1)}) %all-gather.6.cloned.1.call-update) | async-done | bytes 8388624 | tf_op jit(solution)/shard_map/all_gather | solution.py:479
  117.6 27.7 %shard_map.105 = (bf16[128,2048]{1,0:T(8,128)(2,1)}, bf16[2048,128]{1,0:T(8,128)(2,1)}, f32[2048,256]{1,0:T(8,128)}, f32[128,256]{1,0:T(8,128)}, f32[8,64,256]{2,1,0:T(8,128)}) custom-call(s32[2]{0:T(128)} %pad_add_fusion.sibs, bf16[2048,128]{1,0:T(8,128)(2,1)} %get-tuple-element.25.q_ref.dep_ref, bf16[2048,256]{1,0:T(8,128)(2,1)} %get-tuple-element.26.kv_ref, ...), custom_call_target="tpu_custom_call" | custom-call | flops 15300820992 | bytes 8388608 | tf_op jit(solution)/shard_map/pallas_call | solution.py:239
  145.3 5.7 %all-to-all-start.1 = ((f32[8,64,256]{2,1,0:T(8,128)}), f32[8,64,256]{2,1,0:T(8,128)S(1)}, u32[]{:S(2)}, u32[]{:S(2)}) async-start(f32[8,64,256]{2,1,0:T(8,128)} %get-tuple-element.32), calls=%async_computation.1 | async-start | bytes 1048576 | tf_op jit(solution)/shard_map/all_to_all | solution.py:491
  151.7 9.0 %shard_map.106 = (f32[4,4,256,128]{3,2,1,0:T(8,128)}, f32[4,4,256,128]{3,2,1,0:T(8,128)}) custom-call(s32[8]{0:T(128)} %stack.181.chunks, bf16[2048,2048]{1,0:T(8,128)(2,1)} %all-gather.6.cloned.1.call-done.cot_ref.x_ref, bf16[128,2048]{1,0:T(8,128)(2,1)} %get-tuple-element.33.a_ref), custom_call_target="tpu_custom_call" | custom-call | flops 1073741824 | bytes 8388608 | tf_op jit(solution)/shard_map/pallas_call | solution.py:346
  161.6 8.0 %shard_map.107 = (f32[4,4,256,128]{3,2,1,0:T(8,128)}, bf16[2048,384]{1,0:T(8,128)(2,1)}, bf16[384,2048]{1,0:T(8,128)(2,1)}) custom-call(s32[8]{0:T(128)} %stack.181.chunks, s32[2]{0:T(128)} %pad_add_fusion.sibs, bf16[2048,2048]{1,0:T(8,128)(2,1)} %get-tuple-element.24.x_ref, ...), custom_call_target="tpu_custom_call", output_to_operand_aliasing={{0}: (7, {})} | custom-call | flops 1610612736 | bytes 5767168 | tf_op jit(solution)/shard_map/pallas_call | solution.py:409
  170.2 6.6 %shard_map.110 = f32[4,4,256,128]{3,2,1,0:T(8,128)} custom-call(s32[8]{0:T(128)} %stack.181.chunks, bf16[2048,2048]{1,0:T(8,128)(2,1)} %get-tuple-element.24.x_ref, bf16[384,2048]{1,0:T(8,128)(2,1)} %get-tuple-element.40.dt_ref, f32[4,4,256,128]{3,2,1,0:T(8,128)} %get-tuple-element.41.alias_ref), custom_call_target="tpu_custom_call", output_to_operand_aliasing={{}: (3, {})} | custom-call | flops 1610612736 | bytes 5767168 | tf_op jit(solution)/shard_map/pallas_call | solution.py:444
  180.0 4.6 %all-to-all-start.2 = ((bf16[4,512,384]{2,1,0:T(8,128)(2,1)}), bf16[4,512,384]{2,1,0:T(8,128)(2,1)S(1)}, u32[]{:S(2)}, u32[]{:S(2)}) async-start(bf16[4,512,384]{2,1,0:T(8,128)(2,1)} %bitcast.46), calls=%async_computation.2 | async-start | bytes 3145728 | tf_op jit(solution)/shard_map/all_to_all | solution.py:498
  185.2 12.0 %all-to-all-done.2.d_ref = bf16[4,512,384]{2,1,0:T(8,128)(2,1)S(1)} async-done(((bf16[4,512,384]{2,1,0:T(8,128)(2,1)}), bf16[4,512,384]{2,1,0:T(8,128)(2,1)S(1)}, u32[]{:S(2)}, u32[]{:S(2)}) %all-to-all-start.2) | async-done | bytes 1572896 | tf_op jit(solution)/shard_map/all_to_all | solution.py:498
  198.3 8.6 %shard_map.109 = (f32[4,512,128]{2,1,0:T(8,128)}, f32[4,512,128]{2,1,0:T(8,128)}, f32[4,512,128]{2,1,0:T(8,128)}, f32[4,512,128]{2,1,0:T(8,128)}) custom-call(s32[16]{0:T(128)} %stack.172.ids, bf16[4,512,384]{2,1,0:T(8,128)(2,1)} %copy-done.3, bf16[4,2048,384]{2,1,0:T(8,128)(2,1)} %bitcast.56, bf16[4,2048,384]{2,1,0:T(8,128)(2,1)} %bitcast.57, ...), custom_call_target="tpu_custom_call" | custom-call | flops 3221225472 | bytes 10485760 | tf_op jit(solution)/shard_map/pallas_call | solution.py:305
  213.7 22.2 %collective-permute-done.13 = f32[4,512,128]{2,1,0:T(8,128)S(1)} collective-permute-done((f32[4,512,128]{2,1,0:T(8,128)}, f32[4,512,128]{2,1,0:T(8,128)S(1)}, u32[]{:S(2)}, u32[]{:S(2)}) %collective-permute-start.13) | collective-permute-done | bytes 1048608 | tf_op jit(solution)/shard_map/ppermute | solution.py:40
  235.9 3.7 %collective-permute-done.11 = f32[4,512,128]{2,1,0:T(8,128)S(1)} collective-permute-done((f32[4,512,128]{2,1,0:T(8,128)S(1)}, f32[4,512,128]{2,1,0:T(8,128)S(1)}, u32[]{:S(2)}, u32[]{:S(2)}) %collective-permute-start.11) | collective-permute-done | bytes 1048608 | tf_op jit(solution)/shard_map/ppermute | solution.py:40
  239.8 10.9 %all_to_all.20 = bf16[4,512,128]{2,1,0:T(8,128)(2,1)S(1)} all-to-all(bf16[4,512,128]{2,1,0:T(8,128)(2,1)S(1)} %add_convert_fusion), channel_id=1, replica_groups={{0,4,8,12},{1,5,9,13},{2,6,10,14},{3,7,11,15},{16,17,18,19},{20,21,22,2..., dimensions={0} | all-to-all | bytes 1048576 | tf_op jit(solution)/shard_map/all_to_all | solution.py:505
  250.6 3.9 %fusion = (f32[8,1,256,128]{3,2,1,0:T(8,128)S(1)}, f32[8,1,256,128]{3,2,1,0:T(8,128)}, f32[8,1,256,128]{3,2,1,0:T(8,128)}, f32[8,1,256,128]{3,2,1,0:T(8,128)}) fusion(f32[8,4,256,128]{3,2,1,0:T(8,128)} %bitcast.60), kind=kLoop, calls=%fused_computation.7 | loop fusion | bytes 8388608 | tf_op jit(solution)/shard_map/slice | solution.py:471
  (78 shorter events, 35.9 us)
Async XLA Ops:
  7.2 110.4 %all-gather.6.cloned.1.call-start = ((), (), s32[]{:S(2)}) async-start(), calls=%async_computation.5 | async-start | bytes 8912896 | tf_op jit(solution)/shard_map/all_gather | solution.py:479
  9.1 11.5 %collective-permute-start.2 = (bf16[2048,128]{1,0:T(8,128)(2,1)}, bf16[2048,128]{1,0:T(8,128)(2,1)S(1)}, u32[]{:S(2)}, u32[]{:S(2)}) collective-permute-start(bf16[2048,128]{1,0:T(8,128)(2,1)} %param.6), channel_id=1, source_target_pairs={{0,8},{1,9},{2,10},{3,11},{4,12},{5,13},{6,14},{7,15},{8,0},{9,1},... | collective-permute-start | bytes 1572872 | tf_op jit(solution)/shard_map/ppermute | solution.py:40
  13.5 13.3 %collective-permute-start.1 = (bf16[2048,128]{1,0:T(8,128)(2,1)}, bf16[2048,128]{1,0:T(8,128)(2,1)S(1)}, u32[]{:S(2)}, u32[]{:S(2)}) collective-permute-start(bf16[2048,128]{1,0:T(8,128)(2,1)} %param.6), channel_id=1, source_target_pairs={{0,12},{1,13},{2,14},{3,15},{4,0},{5,1},{6,2},{7,3},{8,4},{9,5},{1... | collective-permute-start | bytes 1572872 | tf_op jit(solution)/shard_map/ppermute | solution.py:40
  13.9 14.0 %collective-permute-start = (bf16[2048,128]{1,0:T(8,128)(2,1)}, bf16[2048,128]{1,0:T(8,128)(2,1)S(1)}, u32[]{:S(2)}, u32[]{:S(2)}) collective-permute-start(bf16[2048,128]{1,0:T(8,128)(2,1)} %param.6), channel_id=1, source_target_pairs={{0,4},{1,5},{2,6},{3,7},{4,8},{5,9},{6,10},{7,11},{8,12},{9,13},{1... | collective-permute-start | bytes 1572872 | tf_op jit(solution)/shard_map/ppermute | solution.py:40
  29.5 155.7 %all-gather.8.cloned.1.call-start = ((), (), s32[]{:S(2)}) async-start(), calls=%async_computation.7 | async-start | bytes 7864320 | tf_op jit(solution)/shard_map/all_gather | solution.py:483
  29.5 15.5 %collective-permute-start.3 = (bf16[2,2048,128]{2,1,0:T(8,128)(2,1)}, bf16[2,2048,128]{2,1,0:T(8,128)(2,1)}, u32[]{:S(2)}, u32[]{:S(2)}) collective-permute-start(bf16[2,2048,128]{2,1,0:T(8,128)(2,1)} %shard_map.101.refs_0_), channel_id=1, source_target_pairs={{0,1},{1,2},{2,3},{3,0},{4,5},{5,6},{6,7},{7,4},{8,9},{9,10},{10,1... | collective-permute-start | bytes 3145736 | tf_op jit(solution)/shard_map/ppermute | solution.py:40
  30.8 16.8 %collective-permute-start.6 = (bf16[2,2048,128]{2,1,0:T(8,128)(2,1)S(1)}, bf16[2,2048,128]{2,1,0:T(8,128)(2,1)}, u32[]{:S(2)}, u32[]{:S(2)}) collective-permute-start(bf16[2,2048,128]{2,1,0:T(8,128)(2,1)S(1)} %copy-done.1), channel_id=1, source_target_pairs={{0,3},{1,0},{2,1},{3,2},{4,7},{5,4},{6,5},{7,6},{8,11},{9,8},{10,9... | collective-permute-start | bytes 3145736 | tf_op jit(solution)/shard_map/ppermute | solution.py:40
  33.0 31.7 %collective-permute-start.4 = (bf16[2,2048,128]{2,1,0:T(8,128)(2,1)S(1)}, bf16[2,2048,128]{2,1,0:T(8,128)(2,1)}, u32[]{:S(2)}, u32[]{:S(2)}) collective-permute-start(bf16[2,2048,128]{2,1,0:T(8,128)(2,1)S(1)} %copy-done.1), channel_id=1, source_target_pairs={{0,1},{1,2},{2,3},{3,0},{4,5},{5,6},{6,7},{7,4},{8,9},{9,10},{10,1... | collective-permute-start | bytes 3145736 | tf_op jit(solution)/shard_map/ppermute | solution.py:40
  33.0 31.7 %collective-permute-start.5 = (bf16[2,2048,128]{2,1,0:T(8,128)(2,1)}, bf16[2,2048,128]{2,1,0:T(8,128)(2,1)}, u32[]{:S(2)}, u32[]{:S(2)}) collective-permute-start(bf16[2,2048,128]{2,1,0:T(8,128)(2,1)} %shard_map.101.refs_0_), channel_id=1, source_target_pairs={{0,3},{1,0},{2,1},{3,2},{4,7},{5,4},{6,5},{7,6},{8,11},{9,8},{10,9... | collective-permute-start | bytes 3145736 | tf_op jit(solution)/shard_map/ppermute | solution.py:40
  45.1 30.9 %collective-permute-start.7 = (bf16[2,2048,128]{2,1,0:T(8,128)(2,1)}, bf16[2,2048,128]{2,1,0:T(8,128)(2,1)}, u32[]{:S(2)}, u32[]{:S(2)}) collective-permute-start(bf16[2,2048,128]{2,1,0:T(8,128)(2,1)} %collective-permute-done.3.refs_2_), channel_id=1, source_target_pairs={{0,1},{1,2},{2,3},{3,0},{4,5},{5,6},{6,7},{7,4},{8,9},{9,10},{10,1... | collective-permute-start | bytes 3145736 | tf_op jit(solution)/shard_map/ppermute | solution.py:40
  47.6 34.4 %collective-permute-start.8 = (bf16[2,2048,128]{2,1,0:T(8,128)(2,1)}, bf16[2,2048,128]{2,1,0:T(8,128)(2,1)}, u32[]{:S(2)}, u32[]{:S(2)}) collective-permute-start(bf16[2,2048,128]{2,1,0:T(8,128)(2,1)} %collective-permute-done.6.refs_5_), channel_id=1, source_target_pairs={{0,3},{1,0},{2,1},{3,2},{4,7},{5,4},{6,5},{7,6},{8,11},{9,8},{10,9... | collective-permute-start | bytes 3145736 | tf_op jit(solution)/shard_map/ppermute | solution.py:40
  54.8 27.2 %copy-start.2 = (bf16[2048,384]{1,0:T(8,128)(2,1)}, bf16[2048,384]{1,0:T(8,128)(2,1)S(1)}, u32[]{:S(2)}) copy-start(bf16[2048,384]{1,0:T(8,128)(2,1)S(1)} %constant_dynamic-update-slice_fusion.refs_8_.x_ref) | copy-start | bytes 4718596
  95.2 18.3 %all-to-all-start = ((bf16[8,64,256]{2,1,0:T(8,128)(2,1)}), bf16[8,64,256]{2,1,0:T(8,128)(2,1)S(1)}, u32[]{:S(2)}, u32[]{:S(2)}) async-start(bf16[8,64,256]{2,1,0:T(8,128)(2,1)} %get-tuple-element.28), calls=%async_computation | async-start | bytes 524288 | tf_op jit(solution)/shard_map/all_to_all | solution.py:481
  106.9 1.3 collective-permute-start.9
  145.3 15.5 %all-to-all-start.1 = ((f32[8,64,256]{2,1,0:T(8,128)}), f32[8,64,256]{2,1,0:T(8,128)S(1)}, u32[]{:S(2)}, u32[]{:S(2)}) async-start(f32[8,64,256]{2,1,0:T(8,128)} %get-tuple-element.32), calls=%async_computation.1 | async-start | bytes 1048576 | tf_op jit(solution)/shard_map/all_to_all | solution.py:491
  151.0 59.0 %reduce-scatter.2.cloned.1.call-start = ((), (), s32[]{:S(2)}) async-start(), calls=%async_computation.6 | async-start | bytes 2621440 | tf_op jit(solution)/shard_map/reduce_scatter | solution.py:468
  151.0 9.7 %collective-permute-start.10 = (f32[128,256]{1,0:T(8,128)}, f32[128,256]{1,0:T(8,128)S(1)}, u32[]{:S(2)}, u32[]{:S(2)}) collective-permute-start(f32[128,256]{1,0:T(8,128)} %get-tuple-element.31), channel_id=1, source_target_pairs={{0,16},{16,0},{32,48},{48,32},{64,80},{80,64},{96,112},{112,96},{1... | collective-permute-start | bytes 393224 | tf_op jit(solution)/shard_map/ppermute | solution.py:57
  169.6 7.2 %collective-permute-start.14 = (f32[4,4,256,128]{3,2,1,0:T(8,128)}, f32[4,4,256,128]{3,2,1,0:T(8,128)S(1)}, u32[]{:S(2)}, u32[]{:S(2)}) collective-permute-start(f32[4,4,256,128]{3,2,1,0:T(8,128)} %get-tuple-element.42), channel_id=1, source_target_pairs={{0,16},{16,0},{32,48},{48,32},{64,80},{80,64},{96,112},{112,96},{1... | collective-permute-start | bytes 6291464 | tf_op jit(solution)/shard_map/ppermute | solution.py:57
  180.0 17.2 %all-to-all-start.2 = ((bf16[4,512,384]{2,1,0:T(8,128)(2,1)}), bf16[4,512,384]{2,1,0:T(8,128)(2,1)S(1)}, u32[]{:S(2)}, u32[]{:S(2)}) async-start(bf16[4,512,384]{2,1,0:T(8,128)(2,1)} %bitcast.46), calls=%async_computation.2 | async-start | bytes 3145728 | tf_op jit(solution)/shard_map/all_to_all | solution.py:498
  184.6 66.1 %all-gather.10.cloned.1.call-start = ((), (), s32[]{:S(2)}) async-start(), calls=%async_computation.8 | async-start | bytes 4718592 | tf_op jit(solution)/shard_map/all_gather | solution.py:469
  207.0 32.6 %copy-start.4 = (f32[4,512,128]{2,1,0:T(8,128)S(1)}, f32[4,512,128]{2,1,0:T(8,128)}, u32[]{:S(2)}) copy-start(f32[4,512,128]{2,1,0:T(8,128)} %get-tuple-element.36.dep_ref) | copy-start | bytes 3145732
  210.1 25.8 %collective-permute-start.13 = (f32[4,512,128]{2,1,0:T(8,128)}, f32[4,512,128]{2,1,0:T(8,128)S(1)}, u32[]{:S(2)}, u32[]{:S(2)}) collective-permute-start(f32[4,512,128]{2,1,0:T(8,128)} %get-tuple-element.39), channel_id=1, source_target_pairs={{0,3},{1,0},{2,1},{3,2},{4,7},{5,4},{6,5},{7,6},{8,11},{9,8},{10,9... | collective-permute-start | bytes 3145736 | tf_op jit(solution)/shard_map/ppermute | solution.py:40
  212.5 23.3 %collective-permute-start.12 = (f32[4,512,128]{2,1,0:T(8,128)}, f32[4,512,128]{2,1,0:T(8,128)S(1)}, u32[]{:S(2)}, u32[]{:S(2)}) collective-permute-start(f32[4,512,128]{2,1,0:T(8,128)} %get-tuple-element.38), channel_id=1, source_target_pairs={{0,2},{1,3},{2,0},{3,1},{4,6},{5,7},{6,4},{7,5},{8,10},{9,11},{10,... | collective-permute-start | bytes 3145736 | tf_op jit(solution)/shard_map/ppermute | solution.py:40
  213.1 26.4 %collective-permute-start.11 = (f32[4,512,128]{2,1,0:T(8,128)S(1)}, f32[4,512,128]{2,1,0:T(8,128)S(1)}, u32[]{:S(2)}, u32[]{:S(2)}) collective-permute-start(f32[4,512,128]{2,1,0:T(8,128)S(1)} %copy-done.10), channel_id=1, source_target_pairs={{0,1},{1,2},{2,3},{3,0},{4,5},{5,6},{6,7},{7,4},{8,9},{9,10},{10,1... | collective-permute-start | bytes 3145736 | tf_op jit(solution)/shard_map/ppermute | solution.py:40
  (11 other events, 62.3 us)
Sparse Core Ops, SparseCore 0:
  29.6 87.9 all-gather.5
  119.2 42.1 all-gather.7
  180.1 29.8 reduce-scatter.1
  211.7 32.1 all-gather.9

commit v3 on v2

--- a/solution.py
+++ b/solution.py
@@ -74,7 +74,8 @@
 def gather_features(block):
     up, down, far = [send(block, step, 0) for step in STEPS[1:]]
     near, rest = jnp.stack([block, up]), jnp.stack([down, far])
-    near, rest = after(near, rest), after(rest, near)
+    near = after(near, rest)
+    rest = after(rest, near)
     near_up, rest_down = send(near, 0, 1), send(rest, 0, -1)
     near_down, rest_up = send(near, 0, -1), send(rest, 0, 1)
     near_far, rest_far = send(near_up, 0, 1), send(rest_down, 0, -1)
@@ -321,62 +322,33 @@
     )(ids, d_rows, weights, weights, weights, weights)
 
 
-def chunk_ids():
-    c = lax.axis_index("ctx") % 2
-    return jnp.stack([j * 2 + core for core in (1 - c, c) for j in range(NY)]).astype(jnp.int32)
-
-
-def out_grad_kernel(chunks, x_ref, a_ref, give_ref, keep_ref):
-    step = pl.program_id(0)
+def out_grad_kernel(x_ref, a_ref, out_ref):
     grads = mm(a_ref[...], x_ref[...]).T
-
-    @pl.when(step < NY)
-    def _():
-        give_ref[0, 0] = grads
-
-    @pl.when(step >= NY)
-    def _():
-        keep_ref[0, 0] = grads
-
-
-def out_grads(chunks, cot, attended_t):
+    for i in range(out_ref.shape[0]):
+        out_ref[i, 0] = grads[i * out_ref.shape[2] : (i + 1) * out_ref.shape[2]]
+
+
+def out_grads(cot, attended_t):
     n, f = cot.shape
-    cols = f // (2 * NY)
-    shape = jax.ShapeDtypeStruct((NY, 4, cols, DH), F32)
+    chunk = f // (2 * NY)
     return pl.pallas_call(
         out_grad_kernel,
-        grid_spec=pltpu.PrefetchScalarGridSpec(
-            num_scalar_prefetch=1,
-            grid=(2 * NY,),
-            in_specs=[
-                pl.BlockSpec((n, cols), lambda i, chunks: (0, chunks[i])),
-                pl.BlockSpec((DH, n), lambda i, chunks: (0, 0)),
-            ],
-            out_specs=[
-                pl.BlockSpec(
-                    (1, 1, cols, DH), lambda i, chunks: (jnp.minimum(i, NY - 1), 3, 0, 0)
-                ),
-                pl.BlockSpec(
-                    (1, 1, cols, DH), lambda i, chunks: (jnp.maximum(i - NY, 0), 3, 0, 0)
-                ),
-            ],
-        ),
-        out_shape=[shape, shape],
+        grid=(NY,),
+        in_specs=[
+            pl.BlockSpec((n, 2 * chunk), lambda i: (0, i)),
+            pl.BlockSpec((DH, n), lambda i: (0, 0)),
+        ],
+        out_specs=pl.BlockSpec((2, 1, chunk, DH), lambda i: (i, 3, 0, 0)),
+        out_shape=jax.ShapeDtypeStruct((2 * NY, 4, chunk, DH), F32),
         compiler_params=pltpu.CompilerParams(vmem_limit_bytes=60 * 2**20),
         cost_estimate=pl.CostEstimate(
             flops=2 * n * f * DH, bytes_accessed=2 * n * f, transcendentals=0
         ),
-    )(chunks, cot, attended_t)
-
-
-def store_grads(out_ref, d_t, x):
-    grads = mm(d_t, x).T
-    for i in range(3):
-        out_ref[0, i] = grads[:, i * DH : (i + 1) * DH]
-
-
-def give_kernel(
-    chunks, sibs, x_ref, dq_ref, own_ref, first_ref, others_ref, alias_ref, out_ref, d_ref, dt_ref
+    )(cot, attended_t)
+
+
+def weight_grad_kernel(
+    sibs, x_ref, dq_ref, own_ref, first_ref, others_ref, alias_ref, out_ref, d_ref, dt_ref
 ):
     @pl.when(pl.program_id(0) == 0)
     def _():
@@ -395,80 +367,46 @@
         d_ref[:, DH:] = total.astype(BF)
         dt_ref[...] = d_ref[...].T
 
-    store_grads(out_ref, dt_ref[...], x_ref[...])
-
-
-def keep_kernel(chunks, x_ref, dt_ref, alias_ref, out_ref):
-    store_grads(out_ref, dt_ref[...], x_ref[...])
-
-
-def weight_grads_give(chunks, sibs, feats, d_queries, own, first, others, give):
+    grads = mm(dt_ref[...], x_ref[...]).T
+    chunk = out_ref.shape[2]
+    for i in range(out_ref.shape[0]):
+        for j in range(3):
+            out_ref[i, j] = grads[i * chunk : (i + 1) * chunk, j * DH : (j + 1) * DH]
+
+
+def weight_grads(sibs, feats, d_queries, own, first, others, out):
     n, f = feats.shape
-    cols = f // (2 * NY)
-    whole = lambda i, chunks, sibs: (0, 0)
-    return pl.pallas_call(
-        give_kernel,
-        grid_spec=pltpu.PrefetchScalarGridSpec(
-            num_scalar_prefetch=2,
-            grid=(NY,),
-            in_specs=[
-                pl.BlockSpec((n, cols), lambda i, chunks, sibs: (0, chunks[i])),
-                pl.BlockSpec(d_queries.shape, whole),
-                pl.BlockSpec(own.shape, whole),
-                pl.BlockSpec(first.shape, whole),
-                pl.BlockSpec(others.shape, lambda i, chunks, sibs: (0, 0, 0)),
-                pl.BlockSpec(memory_space=pl.ANY),
-            ],
-            out_specs=[
-                pl.BlockSpec((1, 3, cols, DH), lambda i, chunks, sibs: (i, 0, 0, 0)),
-                pl.BlockSpec((n, 3 * DH), whole),
-                pl.BlockSpec((3 * DH, n), whole),
-            ],
-        ),
-        out_shape=[
-            jax.ShapeDtypeStruct(give.shape, F32),
-            jax.ShapeDtypeStruct((n, 3 * DH), BF),
-            jax.ShapeDtypeStruct((3 * DH, n), BF),
-        ],
-        input_output_aliases={7: 0},
-        compiler_params=pltpu.CompilerParams(vmem_limit_bytes=60 * 2**20),
-        cost_estimate=pl.CostEstimate(
-            flops=3 * n * f * DH, bytes_accessed=n * f + 6 * f * DH, transcendentals=0
-        ),
-    )(chunks, sibs, feats, d_queries, own, first, others, give)
-
-
-def weight_grads_keep(chunks, feats, d_t, keep):
-    n, f = feats.shape
-    cols = f // (2 * NY)
-    return pl.pallas_call(
-        keep_kernel,
+    chunk = f // (2 * NY)
+    whole = lambda i, sibs: (0, 0)
+    return pl.pallas_call(
+        weight_grad_kernel,
         grid_spec=pltpu.PrefetchScalarGridSpec(
             num_scalar_prefetch=1,
             grid=(NY,),
             in_specs=[
-                pl.BlockSpec((n, cols), lambda i, chunks: (0, chunks[NY + i])),
-                pl.BlockSpec(d_t.shape, lambda i, chunks: (0, 0)),
+                pl.BlockSpec((n, 2 * chunk), lambda i, sibs: (0, i)),
+                pl.BlockSpec(d_queries.shape, whole),
+                pl.BlockSpec(own.shape, whole),
+                pl.BlockSpec(first.shape, whole),
+                pl.BlockSpec(others.shape, lambda i, sibs: (0, 0, 0)),
                 pl.BlockSpec(memory_space=pl.ANY),
             ],
-            out_specs=pl.BlockSpec((1, 3, cols, DH), lambda i, chunks: (i, 0, 0, 0)),
-        ),
-        out_shape=jax.ShapeDtypeStruct(keep.shape, F32),
-        input_output_aliases={3: 0},
+            out_specs=[
+                pl.BlockSpec((2, 3, chunk, DH), lambda i, sibs: (i, 0, 0, 0)),
+                pl.BlockSpec((n, 3 * DH), whole),
+            ],
+            scratch_shapes=[pltpu.VMEM((3 * DH, n), BF)],
+        ),
+        out_shape=[
+            jax.ShapeDtypeStruct(out.shape, F32),
+            jax.ShapeDtypeStruct((n, 3 * DH), BF),
+        ],
+        input_output_aliases={6: 0},
         compiler_params=pltpu.CompilerParams(vmem_limit_bytes=60 * 2**20),
         cost_estimate=pl.CostEstimate(
-            flops=3 * n * f * DH, bytes_accessed=n * f + 6 * f * DH, transcendentals=0
-        ),
-    )(chunks, feats, d_t, keep)
-
-
-def sum_ctx(give, keep, dep):
-    halves = keep + send_core(give)
-    columns = [[y * 2 + c for y in range(NY)] for c in range(2)]
-    total = lax.psum_scatter(halves, "ctx", scatter_dimension=0, axis_index_groups=columns)
-    grads = lax.all_gather(after(total, dep), "ctx")
-    rows = grads.shape[0] * grads.shape[2]
-    return [grads[:, i].reshape(rows, DH) for i in range(4)]
+            flops=6 * n * f * DH, bytes_accessed=2 * n * f + 12 * f * DH, transcendentals=0
+        ),
+    )(sibs, feats, d_queries, own, first, others, out)
 
 
 def body(tokens, cotangent, w_query, w_key, w_value, w_out):
@@ -486,25 +424,25 @@
     attended_t, d_queries, d_own, d_first, d_others = attention(
         sibs, queries, keys_values, first, others, cot, w_out
     )
-    chunks = chunk_ids()
-    give, keep = out_grads(chunks, cot, attended_t)
+    grads = out_grads(cot, attended_t)
     d_others = lax.all_to_all(d_others, "ctx", 0, 0)
     d_first = send_core(d_first)
-    give, d_all, d_t = weight_grads_give(
-        chunks, sibs, feats, d_queries, d_own, d_first, d_others, give
-    )
-    keep = weight_grads_keep(chunks, feats, d_t, keep)
+    grads, d_all = weight_grads(sibs, feats, d_queries, d_own, d_first, d_others, grads)
+    grads = lax.psum_scatter(after(grads, weight_heads), "ctx", scatter_dimension=0)
     d_rows = d_all.reshape(NX, own // NX, 3 * DH)
     d_rows = lax.all_to_all(d_rows, ("ctx", "tp"), 0, 0, axis_index_groups=lines)
     parts = token_grad_parts(d_rows, weight_heads)
-    query_grad, key_grad, value_grad, out_grad = sum_ctx(give, keep, parts[0])
+    grads = lax.all_gather(after(grads, parts[0]), "ctx")
+    query_grad, key_grad, value_grad, out_grad = [
+        grads[:, i].reshape(-1, DH) for i in range(4)
+    ]
     out_grad = out_grad.T
     total = parts[0]
     for step in range(1, NZ):
         total = total + send(parts[step], 0, step)
-    token_grad = lax.all_to_all(
-        total.astype(BF), ("ctx", "tp"), 0, 0, axis_index_groups=lines
-    ).reshape(own, DH)
+    total = after(total.astype(BF), grads)
+    token_grad = lax.all_to_all(total, ("ctx", "tp"), 0, 0, axis_index_groups=lines)
+    token_grad = token_grad.reshape(own, DH)
     return (token_grad, query_grad, key_grad, value_grad, out_grad)
 
 

time: 266 us -> 261 us (0.981)
  waiting for transfers between devices: 101 us -> 116 us
  blocking collectives: 10.9 us -> 0 us
  Pallas kernels: 73 us -> 66.3 us
  starting transfers between devices: 43.2 us -> 46.3 us
  local copies, waits for them, and re-layouts: 15.7 us -> 12.9 us
    all_to_all x1 -> x0, blocking collectives: 10.9 us -> none  [body(): lax.all_to_all(total.astype(BF), ('ctx', 'tp'), 0, 0, axis_index_groups=l...]
    pallas_call x3 -> x2, Pallas kernels: 23.6 us -> 16.9 us  [the longest x1 10.7 us: weight_grads(): pl.pallas_call(weight_grad_kernel, grid_spec=pltpu.PrefetchScalarGridSpec...]
    all_gather x1, waiting for transfers between devices: 0.01 us -> 5.27 us  [body(): grads = lax.all_gather(after(grads, parts[0]), 'ctx')]
    all_to_all x0 -> x1, starting transfers between devices: none -> 4.14 us  [body(): lax.all_to_all(total, ('ctx', 'tp'), 0, 0, axis_index_groups=lines)]
    reduce_scatter x1, waiting for transfers between devices: 3.06 us -> 6.87 us  [body(): lax.psum_scatter(after(grads, weight_heads), 'ctx', scatter_dimension=0)]
    add x1 -> x0, other arithmetic: 3.18 us -> none  [sum_ctx(): halves = keep + send_core(give)]
    all_to_all x1, waiting for transfers between devices: 0.01 us -> 3.16 us  [body(): d_others = lax.all_to_all(d_others, 'ctx', 0, 0)]
    unnamed x31 -> x30, local copies, waits for them, and re-layouts: 7.36 us -> 6.22 us
  transfers between devices with their start and end apart: 22 -> 22, of which waited for: 14 -> 17; matrix products, arithmetic and copies ran while one was open for 4% -> 4% of each run, Pallas kernels for 28% -> 26%
where the time goes in v3:
time: 261 us; the launch traced here: 260 us
  waiting for transfers between devices  116 us (44%)
  Pallas kernels  66.3 us (25%)
  starting transfers between devices  46.3 us (18%)
  between operations  13.9 us (5%)
  local copies, waits for them, and re-layouts  12.9 us (5%)
  other arithmetic  4.82 us (2%)
    ppermute x12, waiting for transfers between devices, send(): return lax.ppermute(value, ('ctx', 'tp'), pairs)  75 us
    pallas_call x1, Pallas kernels, attention(): pl.pallas_call(functools.partial(attention_kernel, own, coarse), grid_spe...  27.7 us
    ppermute x12, starting transfers between devices, send(): return lax.ppermute(value, ('ctx', 'tp'), pairs)  20.2 us
    pallas_call x1, Pallas kernels, project(): pl.pallas_call(project_kernel, grid_spec=pltpu.PrefetchScalarGridSpec(num...  13.1 us
    all_to_all x1, waiting for transfers between devices, body(): lax.all_to_all(d_rows, ('ctx', 'tp'), 0, 0, axis_index_groups=lines)  12.2 us
    all_to_all x1, starting transfers between devices, body(): others = lax.all_to_all(others, 'ctx', 0, 0)  11.7 us
    pallas_call x1, Pallas kernels, weight_grads(): pl.pallas_call(weight_grad_kernel, grid_spec=pltpu.PrefetchScalarGridSpec...  10.7 us
    pallas_call x1, Pallas kernels, token_grad_parts(): pl.pallas_call(token_grad_kernel, grid_spec=pltpu.PrefetchScalarGridSpec(...  8.69 us
  transfers between devices with their start and end apart: 22, of which 17 were waited for; matrix products, arithmetic and copies ran while one was open for 4% of the time, Pallas kernels for 26%

profile of v3, /device:TPU:1, one launch (start us, length us, event | category | flops | bytes accessed | tf_op | source)
XLA Modules:
  0.0 259.8 jit_solution(12780271094242138616)
XLA Ops:
  15.6 5.1 %collective-permute-done = bf16[2048,128]{1,0:T(8,128)(2,1)S(1)} collective-permute-done((bf16[2048,128]{1,0:T(8,128)(2,1)}, bf16[2048,128]{1,0:T(8,128)(2,1)S(1)}, u32[]{:S(2)}, u32[]{:S(2)}) %collective-permute-start) | collective-permute-done | bytes 524320 | tf_op jit(solution)/shard_map/ppermute | solution.py:40
  22.8 4.6 %collective-permute-done.2 = bf16[2048,128]{1,0:T(8,128)(2,1)S(1)} collective-permute-done((bf16[2048,128]{1,0:T(8,128)(2,1)}, bf16[2048,128]{1,0:T(8,128)(2,1)S(1)}, u32[]{:S(2)}, u32[]{:S(2)}) %collective-permute-start.2) | collective-permute-done | bytes 524320 | tf_op jit(solution)/shard_map/ppermute | solution.py:40
  35.0 9.9 %collective-permute-done.3.refs_2_ = bf16[2,2048,128]{2,1,0:T(8,128)(2,1)} collective-permute-done((bf16[2,2048,128]{2,1,0:T(8,128)(2,1)S(1)}, bf16[2,2048,128]{2,1,0:T(8,128)(2,1)}, u32[]{:S(2)}, u32[]{:S(2)}) %collective-permute-start.3) | collective-permute-done | bytes 1048608 | tf_op jit(solution)/shard_map/ppermute | solution.py:40
  46.9 3.5 %collective-permute-start.8 = (bf16[2,2048,128]{2,1,0:T(8,128)(2,1)}, bf16[2,2048,128]{2,1,0:T(8,128)(2,1)}, u32[]{:S(2)}, u32[]{:S(2)}) collective-permute-start(bf16[2,2048,128]{2,1,0:T(8,128)(2,1)} %collective-permute-done.6.refs_5_), channel_id=1, source_target_pairs={{0,3},{1,0},{2,1},{3,2},{4,7},{5,4},{6,5},{7,6},{8,11},{9,8},{10,9... | collective-permute-start | bytes 3145736 | tf_op jit(solution)/shard_map/ppermute | solution.py:40
  52.3 12.3 %collective-permute-done.4.refs_3_ = bf16[2,2048,128]{2,1,0:T(8,128)(2,1)} collective-permute-done((bf16[2,2048,128]{2,1,0:T(8,128)(2,1)S(1)}, bf16[2,2048,128]{2,1,0:T(8,128)(2,1)}, u32[]{:S(2)}, u32[]{:S(2)}) %collective-permute-start.4) | collective-permute-done | bytes 1048608 | tf_op jit(solution)/shard_map/ppermute | solution.py:40
  64.6 12.2 %collective-permute-done.7.refs_6_ = bf16[2,2048,128]{2,1,0:T(8,128)(2,1)} collective-permute-done((bf16[2,2048,128]{2,1,0:T(8,128)(2,1)}, bf16[2,2048,128]{2,1,0:T(8,128)(2,1)}, u32[]{:S(2)}, u32[]{:S(2)}) %collective-permute-start.7) | collective-permute-done | bytes 1048608 | tf_op jit(solution)/shard_map/ppermute | solution.py:40
  76.8 4.5 %collective-permute-done.8.refs_7_ = bf16[2,2048,128]{2,1,0:T(8,128)(2,1)} collective-permute-done((bf16[2,2048,128]{2,1,0:T(8,128)(2,1)}, bf16[2,2048,128]{2,1,0:T(8,128)(2,1)}, u32[]{:S(2)}, u32[]{:S(2)}) %collective-permute-start.8) | collective-permute-done | bytes 1048608 | tf_op jit(solution)/shard_map/ppermute | solution.py:40
  81.3 13.1 %shard_map.103 = (bf16[2048,2048]{1,0:T(8,128)(2,1)}, bf16[2048,128]{1,0:T(8,128)(2,1)}, bf16[2048,256]{1,0:T(8,128)(2,1)}, bf16[128,256]{1,0:T(8,128)(2,1)}, bf16[8,64,256]{2,1,0:T(8,128)(2,1)}) custom-call(s32[16]{0:T(128)} %stack.165.ids, s32[2]{0:T(128)} %pad_add_fusion.sibs, bf16[2,2048,128]{2,1,0:T(8,128)(2,1)} %shard_map.101.dep_ref.refs_0_, ...), custom_call_target="tpu_custom_call" | custom-call | flops 3221225472 | bytes 16777216 | tf_op jit(solution)/shard_map/pallas_call | solution.py:140
  94.4 11.7 %all-to-all-start = ((bf16[8,64,256]{2,1,0:T(8,128)(2,1)}), bf16[8,64,256]{2,1,0:T(8,128)(2,1)S(1)}, u32[]{:S(2)}, u32[]{:S(2)}) async-start(bf16[8,64,256]{2,1,0:T(8,128)(2,1)} %get-tuple-element.25), calls=%async_computation | async-start | bytes 524288 | tf_op jit(solution)/shard_map/all_to_all | solution.py:419
  107.4 5.3 %all-to-all-done.others_ref = bf16[8,64,256]{2,1,0:T(8,128)(2,1)S(1)} async-done(((bf16[8,64,256]{2,1,0:T(8,128)(2,1)}), bf16[8,64,256]{2,1,0:T(8,128)(2,1)S(1)}, u32[]{:S(2)}, u32[]{:S(2)}) %all-to-all-start) | async-done | bytes 262176 | tf_op jit(solution)/shard_map/all_to_all | solution.py:419
  112.7 4.7 %all-gather.6.cloned.1.call-done.cot_ref.x_ref = bf16[2048,2048]{1,0:T(8,128)(2,1)} async-done(((bf16[2048,128]{1,0:T(8,128)(2,1)}), bf16[2048,2048]{1,0:T(8,128)(2,1)}) %all-gather.6.cloned.1.call-update) | async-done | bytes 8388624 | tf_op jit(solution)/shard_map/all_gather | solution.py:417
  117.4 27.7 %shard_map.105 = (bf16[128,2048]{1,0:T(8,128)(2,1)}, bf16[2048,128]{1,0:T(8,128)(2,1)}, f32[2048,256]{1,0:T(8,128)}, f32[128,256]{1,0:T(8,128)}, f32[8,64,256]{2,1,0:T(8,128)}) custom-call(s32[2]{0:T(128)} %pad_add_fusion.sibs, bf16[2048,128]{1,0:T(8,128)(2,1)} %get-tuple-element.22.q_ref.dep_ref, bf16[2048,256]{1,0:T(8,128)(2,1)} %get-tuple-element.23.kv_ref, ...), custom_call_target="tpu_custom_call" | custom-call | flops 15300820992 | bytes 8388608 | tf_op jit(solution)/shard_map/pallas_call | solution.py:240
  145.0 5.7 %all-to-all-start.1 = ((f32[8,64,256]{2,1,0:T(8,128)}), f32[8,64,256]{2,1,0:T(8,128)S(1)}, u32[]{:S(2)}, u32[]{:S(2)}) async-start(f32[8,64,256]{2,1,0:T(8,128)} %get-tuple-element.29), calls=%async_computation.1 | async-start | bytes 1048576 | tf_op jit(solution)/shard_map/all_to_all | solution.py:428
  150.9 6.2 %shard_map.106.alias_ref = f32[8,4,256,128]{3,2,1,0:T(8,128)} custom-call(bf16[2048,2048]{1,0:T(8,128)(2,1)} %all-gather.6.cloned.1.call-done.cot_ref.x_ref, bf16[128,2048]{1,0:T(8,128)(2,1)} %get-tuple-element.30.a_ref), custom_call_target="tpu_custom_call" | custom-call | flops 1073741824 | bytes 8388608 | tf_op jit(solution)/shard_map/pallas_call | solution.py:334
  161.0 10.7 %shard_map.107 = (f32[8,4,256,128]{3,2,1,0:T(8,128)}, bf16[2048,384]{1,0:T(8,128)(2,1)}) custom-call(s32[2]{0:T(128)} %pad_add_fusion.sibs, bf16[2048,2048]{1,0:T(8,128)(2,1)} %get-tuple-element.21.x_ref, bf16[2048,128]{1,0:T(8,128)(2,1)} %get-tuple-element.26.dq_ref, f32[2048,256]{1,0:T(8,128)} %get-tuple-element.27.own_ref, ...), custom_call_target="tpu_custom_call", output_to_operand_aliasing={{0}: (6, {})} | custom-call | flops 3221225472 | bytes 11534336 | tf_op jit(solution)/shard_map/pallas_call | solution.py:381
  171.8 4.0 %all-to-all-start.2 = ((bf16[4,512,384]{2,1,0:T(8,128)(2,1)}), bf16[4,512,384]{2,1,0:T(8,128)(2,1)S(1)}, u32[]{:S(2)}, u32[]{:S(2)}) async-start(bf16[4,512,384]{2,1,0:T(8,128)(2,1)} %bitcast.58), calls=%async_computation.2 | async-start | bytes 3145728 | tf_op jit(solution)/shard_map/all_to_all | solution.py:433
  176.5 12.2 %all-to-all-done.2.d_ref = bf16[4,512,384]{2,1,0:T(8,128)(2,1)S(1)} async-done(((bf16[4,512,384]{2,1,0:T(8,128)(2,1)}), bf16[4,512,384]{2,1,0:T(8,128)(2,1)S(1)}, u32[]{:S(2)}, u32[]{:S(2)}) %all-to-all-start.2) | async-done | bytes 1572896 | tf_op jit(solution)/shard_map/all_to_all | solution.py:433
  189.8 8.7 %shard_map.109 = (f32[4,512,128]{2,1,0:T(8,128)}, f32[4,512,128]{2,1,0:T(8,128)}, f32[4,512,128]{2,1,0:T(8,128)}, f32[4,512,128]{2,1,0:T(8,128)}) custom-call(s32[16]{0:T(128)} %stack.145.ids, bf16[4,512,384]{2,1,0:T(8,128)(2,1)} %copy-done.3, bf16[4,2048,384]{2,1,0:T(8,128)(2,1)} %bitcast.49, bf16[4,2048,384]{2,1,0:T(8,128)(2,1)} %bitcast.50, ...), custom_call_target="tpu_custom_call" | custom-call | flops 3221225472 | bytes 10485760 | tf_op jit(solution)/shard_map/pallas_call | solution.py:306
  198.5 6.9 %reduce-scatter.2.cloned.1.call-done = f32[1,4,256,128]{3,2,1,0:T(8,128)} async-done(((f32[8,4,256,128]{3,2,1,0:T(8,128)}), f32[1,4,256,128]{3,2,1,0:T(8,128)}) %reduce-scatter.2.cloned.1.call-update) | async-done | bytes 524304 | tf_op jit(solution)/shard_map/reduce_scatter | solution.py:431
  208.7 22.4 %collective-permute-done.13 = f32[4,512,128]{2,1,0:T(8,128)S(1)} collective-permute-done((f32[4,512,128]{2,1,0:T(8,128)}, f32[4,512,128]{2,1,0:T(8,128)S(1)}, u32[]{:S(2)}, u32[]{:S(2)}) %collective-permute-start.13) | collective-permute-done | bytes 1048608 | tf_op jit(solution)/shard_map/ppermute | solution.py:40
  231.1 3.7 %collective-permute-done.11 = f32[4,512,128]{2,1,0:T(8,128)S(1)} collective-permute-done((f32[4,512,128]{2,1,0:T(8,128)}, f32[4,512,128]{2,1,0:T(8,128)S(1)}, u32[]{:S(2)}, u32[]{:S(2)}) %collective-permute-start.11) | collective-permute-done | bytes 1048608 | tf_op jit(solution)/shard_map/ppermute | solution.py:40
  235.8 5.3 %all-gather.10.cloned.1.call-done = f32[32,256,128]{2,1,0:T(8,128)} async-done(((f32[4,256,128]{2,1,0:T(8,128)}), f32[32,256,128]{2,1,0:T(8,128)}) %all-gather.10.cloned.1.call-update) | async-done | bytes 4194320 | tf_op jit(solution)/shard_map/all_gather | solution.py:435
  241.1 4.1 %all-to-all-start.3 = ((bf16[4,512,128]{2,1,0:T(8,128)(2,1)}), bf16[4,512,128]{2,1,0:T(8,128)(2,1)S(1)}, u32[]{:S(2)}, u32[]{:S(2)}) async-start(bf16[4,512,128]{2,1,0:T(8,128)(2,1)} %shard_map.112), calls=%async_computation.4 | async-start | bytes 1048576 | tf_op jit(solution)/shard_map/all_to_all | solution.py:444
  245.2 3.9 %fusion = (f32[8,1,256,128]{3,2,1,0:T(8,128)S(1)}, f32[8,1,256,128]{3,2,1,0:T(8,128)}, f32[8,1,256,128]{3,2,1,0:T(8,128)}, f32[8,1,256,128]{3,2,1,0:T(8,128)}) fusion(f32[8,4,256,128]{3,2,1,0:T(8,128)} %bitcast.54), kind=kLoop, calls=%fused_computation.7 | loop fusion | bytes 8388608 | tf_op jit(solution)/shard_map/slice | solution.py:437
  (75 shorter events, 37.7 us)
Async XLA Ops:
  7.2 110.2 %all-gather.6.cloned.1.call-start = ((), (), s32[]{:S(2)}) async-start(), calls=%async_computation.5 | async-start | bytes 8912896 | tf_op jit(solution)/shard_map/all_gather | solution.py:417
  9.1 11.6 %collective-permute-start = (bf16[2048,128]{1,0:T(8,128)(2,1)}, bf16[2048,128]{1,0:T(8,128)(2,1)S(1)}, u32[]{:S(2)}, u32[]{:S(2)}) collective-permute-start(bf16[2048,128]{1,0:T(8,128)(2,1)} %param.6), channel_id=1, source_target_pairs={{0,4},{1,5},{2,6},{3,7},{4,8},{5,9},{6,10},{7,11},{8,12},{9,13},{1... | collective-permute-start | bytes 1572872 | tf_op jit(solution)/shard_map/ppermute | solution.py:40
  11.5 15.8 %collective-permute-start.2 = (bf16[2048,128]{1,0:T(8,128)(2,1)}, bf16[2048,128]{1,0:T(8,128)(2,1)S(1)}, u32[]{:S(2)}, u32[]{:S(2)}) collective-permute-start(bf16[2048,128]{1,0:T(8,128)(2,1)} %param.6), channel_id=1, source_target_pairs={{0,8},{1,9},{2,10},{3,11},{4,12},{5,13},{6,14},{7,15},{8,0},{9,1},... | collective-permute-start | bytes 1572872 | tf_op jit(solution)/shard_map/ppermute | solution.py:40
  14.8 12.5 %collective-permute-start.1 = (bf16[2048,128]{1,0:T(8,128)(2,1)}, bf16[2048,128]{1,0:T(8,128)(2,1)S(1)}, u32[]{:S(2)}, u32[]{:S(2)}) collective-permute-start(bf16[2048,128]{1,0:T(8,128)(2,1)} %param.6), channel_id=1, source_target_pairs={{0,12},{1,13},{2,14},{3,15},{4,0},{5,1},{6,2},{7,3},{8,4},{9,5},{1... | collective-permute-start | bytes 1572872 | tf_op jit(solution)/shard_map/ppermute | solution.py:40
  28.5 23.4 %copy-start.7 = (bf16[2048,128]{1,0:T(8,128)(2,1)S(1)}, bf16[2048,128]{1,0:T(8,128)(2,1)}, u32[]{:S(2)}) copy-start(bf16[2048,128]{1,0:T(8,128)(2,1)} %param.9) | copy-start | bytes 1572868
  28.5 143.2 %all-gather.8.cloned.1.call-start = ((), (), s32[]{:S(2)}) async-start(), calls=%async_computation.7 | async-start | bytes 7864320 | tf_op jit(solution)/shard_map/all_gather | solution.py:421
  29.7 15.3 %collective-permute-start.3 = (bf16[2,2048,128]{2,1,0:T(8,128)(2,1)S(1)}, bf16[2,2048,128]{2,1,0:T(8,128)(2,1)}, u32[]{:S(2)}, u32[]{:S(2)}) collective-permute-start(bf16[2,2048,128]{2,1,0:T(8,128)(2,1)S(1)} %copy-done.1), channel_id=1, source_target_pairs={{0,1},{1,2},{2,3},{3,0},{4,5},{5,6},{6,7},{7,4},{8,9},{9,10},{10,1... | collective-permute-start | bytes 3145736 | tf_op jit(solution)/shard_map/ppermute | solution.py:40
  30.8 16.2 %collective-permute-start.6 = (bf16[2,2048,128]{2,1,0:T(8,128)(2,1)S(1)}, bf16[2,2048,128]{2,1,0:T(8,128)(2,1)}, u32[]{:S(2)}, u32[]{:S(2)}) collective-permute-start(bf16[2,2048,128]{2,1,0:T(8,128)(2,1)S(1)} %copy-done), channel_id=1, source_target_pairs={{0,3},{1,0},{2,1},{3,2},{4,7},{5,4},{6,5},{7,6},{8,11},{9,8},{10,9... | collective-permute-start | bytes 3145736 | tf_op jit(solution)/shard_map/ppermute | solution.py:40
  32.4 32.2 %collective-permute-start.4 = (bf16[2,2048,128]{2,1,0:T(8,128)(2,1)S(1)}, bf16[2,2048,128]{2,1,0:T(8,128)(2,1)}, u32[]{:S(2)}, u32[]{:S(2)}) collective-permute-start(bf16[2,2048,128]{2,1,0:T(8,128)(2,1)S(1)} %copy-done), channel_id=1, source_target_pairs={{0,1},{1,2},{2,3},{3,0},{4,5},{5,6},{6,7},{7,4},{8,9},{9,10},{10,1... | collective-permute-start | bytes 3145736 | tf_op jit(solution)/shard_map/ppermute | solution.py:40
  32.4 32.2 %collective-permute-start.5 = (bf16[2,2048,128]{2,1,0:T(8,128)(2,1)S(1)}, bf16[2,2048,128]{2,1,0:T(8,128)(2,1)}, u32[]{:S(2)}, u32[]{:S(2)}) collective-permute-start(bf16[2,2048,128]{2,1,0:T(8,128)(2,1)S(1)} %copy-done.1), channel_id=1, source_target_pairs={{0,3},{1,0},{2,1},{3,2},{4,7},{5,4},{6,5},{7,6},{8,11},{9,8},{10,9... | collective-permute-start | bytes 3145736 | tf_op jit(solution)/shard_map/ppermute | solution.py:40
  44.9 31.9 %collective-permute-start.7 = (bf16[2,2048,128]{2,1,0:T(8,128)(2,1)}, bf16[2,2048,128]{2,1,0:T(8,128)(2,1)}, u32[]{:S(2)}, u32[]{:S(2)}) collective-permute-start(bf16[2,2048,128]{2,1,0:T(8,128)(2,1)} %collective-permute-done.3.refs_2_), channel_id=1, source_target_pairs={{0,1},{1,2},{2,3},{3,0},{4,5},{5,6},{6,7},{7,4},{8,9},{9,10},{10,1... | collective-permute-start | bytes 3145736 | tf_op jit(solution)/shard_map/ppermute | solution.py:40
  46.9 34.4 %collective-permute-start.8 = (bf16[2,2048,128]{2,1,0:T(8,128)(2,1)}, bf16[2,2048,128]{2,1,0:T(8,128)(2,1)}, u32[]{:S(2)}, u32[]{:S(2)}) collective-permute-start(bf16[2,2048,128]{2,1,0:T(8,128)(2,1)} %collective-permute-done.6.refs_5_), channel_id=1, source_target_pairs={{0,3},{1,0},{2,1},{3,2},{4,7},{5,4},{6,5},{7,6},{8,11},{9,8},{10,9... | collective-permute-start | bytes 3145736 | tf_op jit(solution)/shard_map/ppermute | solution.py:40
  94.4 18.2 %all-to-all-start = ((bf16[8,64,256]{2,1,0:T(8,128)(2,1)}), bf16[8,64,256]{2,1,0:T(8,128)(2,1)S(1)}, u32[]{:S(2)}, u32[]{:S(2)}) async-start(bf16[8,64,256]{2,1,0:T(8,128)(2,1)} %get-tuple-element.25), calls=%async_computation | async-start | bytes 524288 | tf_op jit(solution)/shard_map/all_to_all | solution.py:419
  106.1 1.3 collective-permute-start.9
  145.0 15.2 %all-to-all-start.1 = ((f32[8,64,256]{2,1,0:T(8,128)}), f32[8,64,256]{2,1,0:T(8,128)S(1)}, u32[]{:S(2)}, u32[]{:S(2)}) async-start(f32[8,64,256]{2,1,0:T(8,128)} %get-tuple-element.29), calls=%async_computation.1 | async-start | bytes 1048576 | tf_op jit(solution)/shard_map/all_to_all | solution.py:428
  150.8 54.6 %reduce-scatter.2.cloned.1.call-start = ((), (), s32[]{:S(2)}) async-start(), calls=%async_computation.6 | async-start | bytes 4718592 | tf_op jit(solution)/shard_map/reduce_scatter | solution.py:431
  150.8 6.3 %collective-permute-start.10 = (f32[128,256]{1,0:T(8,128)}, f32[128,256]{1,0:T(8,128)S(1)}, u32[]{:S(2)}, u32[]{:S(2)}) collective-permute-start(f32[128,256]{1,0:T(8,128)} %get-tuple-element.28), channel_id=1, source_target_pairs={{0,16},{16,0},{32,48},{48,32},{64,80},{80,64},{96,112},{112,96},{1... | collective-permute-start | bytes 393224 | tf_op jit(solution)/shard_map/ppermute | solution.py:57
  171.8 16.9 %all-to-all-start.2 = ((bf16[4,512,384]{2,1,0:T(8,128)(2,1)}), bf16[4,512,384]{2,1,0:T(8,128)(2,1)S(1)}, u32[]{:S(2)}, u32[]{:S(2)}) async-start(bf16[4,512,384]{2,1,0:T(8,128)(2,1)} %bitcast.58), calls=%async_computation.2 | async-start | bytes 3145728 | tf_op jit(solution)/shard_map/all_to_all | solution.py:433
  175.8 65.3 %all-gather.10.cloned.1.call-start = ((), (), s32[]{:S(2)}) async-start(), calls=%async_computation.8 | async-start | bytes 4718592 | tf_op jit(solution)/shard_map/all_gather | solution.py:435
  198.5 36.2 %copy-start.4 = (f32[4,512,128]{2,1,0:T(8,128)S(1)}, f32[4,512,128]{2,1,0:T(8,128)}, u32[]{:S(2)}) copy-start(f32[4,512,128]{2,1,0:T(8,128)} %get-tuple-element.32.dep_ref) | copy-start | bytes 3145732
  205.4 25.7 %collective-permute-start.13 = (f32[4,512,128]{2,1,0:T(8,128)}, f32[4,512,128]{2,1,0:T(8,128)S(1)}, u32[]{:S(2)}, u32[]{:S(2)}) collective-permute-start(f32[4,512,128]{2,1,0:T(8,128)} %get-tuple-element.35), channel_id=1, source_target_pairs={{0,3},{1,0},{2,1},{3,2},{4,7},{5,4},{6,5},{7,6},{8,11},{9,8},{10,9... | collective-permute-start | bytes 3145736 | tf_op jit(solution)/shard_map/ppermute | solution.py:40
  207.8 23.3 %collective-permute-start.12 = (f32[4,512,128]{2,1,0:T(8,128)}, f32[4,512,128]{2,1,0:T(8,128)S(1)}, u32[]{:S(2)}, u32[]{:S(2)}) collective-permute-start(f32[4,512,128]{2,1,0:T(8,128)} %get-tuple-element.34), channel_id=1, source_target_pairs={{0,2},{1,3},{2,0},{3,1},{4,6},{5,7},{6,4},{7,5},{8,10},{9,11},{10,... | collective-permute-start | bytes 3145736 | tf_op jit(solution)/shard_map/ppermute | solution.py:40
  208.2 26.6 %collective-permute-start.11 = (f32[4,512,128]{2,1,0:T(8,128)}, f32[4,512,128]{2,1,0:T(8,128)S(1)}, u32[]{:S(2)}, u32[]{:S(2)}) collective-permute-start(f32[4,512,128]{2,1,0:T(8,128)} %get-tuple-element.33), channel_id=1, source_target_pairs={{0,1},{1,2},{2,3},{3,0},{4,5},{5,6},{6,7},{7,4},{8,9},{9,10},{10,1... | collective-permute-start | bytes 3145736 | tf_op jit(solution)/shard_map/ppermute | solution.py:40
  241.1 11.4 %all-to-all-start.3 = ((bf16[4,512,128]{2,1,0:T(8,128)(2,1)}), bf16[4,512,128]{2,1,0:T(8,128)(2,1)S(1)}, u32[]{:S(2)}, u32[]{:S(2)}) async-start(bf16[4,512,128]{2,1,0:T(8,128)(2,1)} %shard_map.112), calls=%async_computation.4 | async-start | bytes 1048576 | tf_op jit(solution)/shard_map/all_to_all | solution.py:444
  (11 other events, 71.7 us)
Sparse Core Ops, SparseCore 0:
  28.6 88.6 all-gather.5
  119.0 41.5 all-gather.7
  171.9 33.4 reduce-scatter.1
  207.0 34.0 all-gather.9

commit v4 on v3

--- a/solution.py
+++ b/solution.py
@@ -414,7 +414,8 @@
     ids, sibs, lines = block_ids(), sibling_ids(), first_lines()
     weights = jnp.concatenate([w_query, w_key, w_value], axis=1)
     tok_parts = gather_features(tokens)
-    cot = lax.all_gather(after(cotangent, tok_parts[1]), "tp", axis=1, tiled=True)
+    ordered = cotangent + tok_parts[1][0, 0, 0] * 0
+    cot = lax.all_gather(ordered, "tp", axis=1, tiled=True)
     feats, queries, keys_values, first, others = project(ids, sibs, tok_parts, weights)
     others = lax.all_to_all(others, "ctx", 0, 0)
     first = send_core(first)

time: 261 us -> 261 us (level)
    unnamed x30 -> x29, local copies, waits for them, and re-layouts: 6.22 us -> 3.03 us
  transfers between devices with their start and end apart: 22 -> 22, of which waited for: 17 -> 18; matrix products, arithmetic and copies ran while one was open for 4% -> 5% of each run, Pallas kernels for 26% -> 26%
where the time goes in v4:
time: 261 us; the launch traced here: 260 us
  waiting for transfers between devices  118 us (45%)
  Pallas kernels  66.3 us (25%)
  starting transfers between devices  43.8 us (17%)
  between operations  14.5 us (6%)
  local copies, waits for them, and re-layouts  12.2 us (5%)
  other arithmetic  5.67 us (2%)
    ppermute x12, waiting for transfers between devices, send(): return lax.ppermute(value, ('ctx', 'tp'), pairs)  74.3 us
    pallas_call x1, Pallas kernels, attention(): pl.pallas_call(functools.partial(attention_kernel, own, coarse), grid_spe...  27.7 us
    ppermute x12, starting transfers between devices, send(): return lax.ppermute(value, ('ctx', 'tp'), pairs)  18.7 us
    pallas_call x1, Pallas kernels, project(): pl.pallas_call(project_kernel, grid_spec=pltpu.PrefetchScalarGridSpec(num...  13 us
    all_to_all x1, waiting for transfers between devices, body(): lax.all_to_all(d_rows, ('ctx', 'tp'), 0, 0, axis_index_groups=lines)  12.2 us
    all_to_all x1, starting transfers between devices, body(): others = lax.all_to_all(others, 'ctx', 0, 0)  11 us
    pallas_call x1, Pallas kernels, weight_grads(): pl.pallas_call(weight_grad_kernel, grid_spec=pltpu.PrefetchScalarGridSpec...  10.7 us
    pallas_call x1, Pallas kernels, token_grad_parts(): pl.pallas_call(token_grad_kernel, grid_spec=pltpu.PrefetchScalarGridSpec(...  8.69 us
  transfers between devices with their start and end apart: 22, of which 18 were waited for; matrix products, arithmetic and copies ran while one was open for 5% of the time, Pallas kernels for 26%

profile of v4, /device:TPU:1, one launch (start us, length us, event | category | flops | bytes accessed | tf_op | source)
XLA Modules:
  0.0 259.9 jit_solution(11991120038079091606)
XLA Ops:
  13.8 5.1 %collective-permute-done = bf16[2048,128]{1,0:T(8,128)(2,1)S(1)} collective-permute-done((bf16[2048,128]{1,0:T(8,128)(2,1)}, bf16[2048,128]{1,0:T(8,128)(2,1)S(1)}, u32[]{:S(2)}, u32[]{:S(2)}) %collective-permute-start) | collective-permute-done | bytes 524320 | tf_op jit(solution)/shard_map/ppermute | solution.py:40
  21.0 4.6 %collective-permute-done.2 = bf16[2048,128]{1,0:T(8,128)(2,1)S(1)} collective-permute-done((bf16[2048,128]{1,0:T(8,128)(2,1)}, bf16[2048,128]{1,0:T(8,128)(2,1)S(1)}, u32[]{:S(2)}, u32[]{:S(2)}) %collective-permute-start.2) | collective-permute-done | bytes 524320 | tf_op jit(solution)/shard_map/ppermute | solution.py:40
  35.0 9.9 %collective-permute-done.3.refs_2_ = bf16[2,2048,128]{2,1,0:T(8,128)(2,1)} collective-permute-done((bf16[2,2048,128]{2,1,0:T(8,128)(2,1)S(1)}, bf16[2,2048,128]{2,1,0:T(8,128)(2,1)}, u32[]{:S(2)}, u32[]{:S(2)}) %collective-permute-start.3) | collective-permute-done | bytes 1048608 | tf_op jit(solution)/shard_map/ppermute | solution.py:40
  47.2 3.4 %collective-permute-start.8 = (bf16[2,2048,128]{2,1,0:T(8,128)(2,1)}, bf16[2,2048,128]{2,1,0:T(8,128)(2,1)}, u32[]{:S(2)}, u32[]{:S(2)}) collective-permute-start(bf16[2,2048,128]{2,1,0:T(8,128)(2,1)} %collective-permute-done.6.refs_5_), channel_id=1, source_target_pairs={{0,3},{1,0},{2,1},{3,2},{4,7},{5,4},{6,5},{7,6},{8,11},{9,8},{10,9... | collective-permute-start | bytes 3145736 | tf_op jit(solution)/shard_map/ppermute | solution.py:40
  53.4 11.2 %collective-permute-done.4.refs_3_ = bf16[2,2048,128]{2,1,0:T(8,128)(2,1)} collective-permute-done((bf16[2,2048,128]{2,1,0:T(8,128)(2,1)}, bf16[2,2048,128]{2,1,0:T(8,128)(2,1)}, u32[]{:S(2)}, u32[]{:S(2)}) %collective-permute-start.4) | collective-permute-done | bytes 1048608 | tf_op jit(solution)/shard_map/ppermute | solution.py:40
  64.7 11.2 %collective-permute-done.7.refs_6_ = bf16[2,2048,128]{2,1,0:T(8,128)(2,1)} collective-permute-done((bf16[2,2048,128]{2,1,0:T(8,128)(2,1)}, bf16[2,2048,128]{2,1,0:T(8,128)(2,1)}, u32[]{:S(2)}, u32[]{:S(2)}) %collective-permute-start.7) | collective-permute-done | bytes 1048608 | tf_op jit(solution)/shard_map/ppermute | solution.py:40
  75.8 4.0 %collective-permute-done.8.refs_7_ = bf16[2,2048,128]{2,1,0:T(8,128)(2,1)} collective-permute-done((bf16[2,2048,128]{2,1,0:T(8,128)(2,1)}, bf16[2,2048,128]{2,1,0:T(8,128)(2,1)}, u32[]{:S(2)}, u32[]{:S(2)}) %collective-permute-start.8) | collective-permute-done | bytes 1048608 | tf_op jit(solution)/shard_map/ppermute | solution.py:40
  79.8 13.0 %shard_map.103 = (bf16[2048,2048]{1,0:T(8,128)(2,1)}, bf16[2048,128]{1,0:T(8,128)(2,1)}, bf16[2048,256]{1,0:T(8,128)(2,1)}, bf16[128,256]{1,0:T(8,128)(2,1)}, bf16[8,64,256]{2,1,0:T(8,128)(2,1)}) custom-call(s32[16]{0:T(128)} %stack.165.ids, s32[2]{0:T(128)} %pad_add_fusion.sibs, bf16[2,2048,128]{2,1,0:T(8,128)(2,1)} %shard_map.101.dep_ref.refs_0_, ...), custom_call_target="tpu_custom_call" | custom-call | flops 3221225472 | bytes 16777216 | tf_op jit(solution)/shard_map/pallas_call | solution.py:140
  92.9 11.0 %all-to-all-start = ((bf16[8,64,256]{2,1,0:T(8,128)(2,1)}), bf16[8,64,256]{2,1,0:T(8,128)(2,1)S(1)}, u32[]{:S(2)}, u32[]{:S(2)}) async-start(bf16[8,64,256]{2,1,0:T(8,128)(2,1)} %get-tuple-element.25), calls=%async_computation | async-start | bytes 524288 | tf_op jit(solution)/shard_map/all_to_all | solution.py:420
  105.2 5.3 %all-to-all-done.others_ref = bf16[8,64,256]{2,1,0:T(8,128)(2,1)S(1)} async-done(((bf16[8,64,256]{2,1,0:T(8,128)(2,1)}), bf16[8,64,256]{2,1,0:T(8,128)(2,1)S(1)}, u32[]{:S(2)}, u32[]{:S(2)}) %all-to-all-start) | async-done | bytes 262176 | tf_op jit(solution)/shard_map/all_to_all | solution.py:420
  110.5 7.2 %all-gather.6.cloned.1.call-done.cot_ref.x_ref = bf16[2048,2048]{1,0:T(8,128)(2,1)} async-done(((bf16[2048,128]{1,0:T(8,128)(2,1)}), bf16[2048,2048]{1,0:T(8,128)(2,1)}) %all-gather.6.cloned.1.call-update) | async-done | bytes 8388624 | tf_op jit(solution)/shard_map/all_gather | solution.py:418
  117.7 27.7 %shard_map.104 = (bf16[128,2048]{1,0:T(8,128)(2,1)}, bf16[2048,128]{1,0:T(8,128)(2,1)}, f32[2048,256]{1,0:T(8,128)}, f32[128,256]{1,0:T(8,128)}, f32[8,64,256]{2,1,0:T(8,128)}) custom-call(s32[2]{0:T(128)} %pad_add_fusion.sibs, bf16[2048,128]{1,0:T(8,128)(2,1)} %get-tuple-element.22.q_ref.dep_ref, bf16[2048,256]{1,0:T(8,128)(2,1)} %get-tuple-element.23.kv_ref, ...), custom_call_target="tpu_custom_call" | custom-call | flops 15300820992 | bytes 8388608 | tf_op jit(solution)/shard_map/pallas_call | solution.py:240
  145.3 5.5 %all-to-all-start.1 = ((f32[8,64,256]{2,1,0:T(8,128)}), f32[8,64,256]{2,1,0:T(8,128)S(1)}, u32[]{:S(2)}, u32[]{:S(2)}) async-start(f32[8,64,256]{2,1,0:T(8,128)} %get-tuple-element.29), calls=%async_computation.1 | async-start | bytes 1048576 | tf_op jit(solution)/shard_map/all_to_all | solution.py:429
  150.9 6.2 %shard_map.105.alias_ref = f32[8,4,256,128]{3,2,1,0:T(8,128)} custom-call(bf16[2048,2048]{1,0:T(8,128)(2,1)} %all-gather.6.cloned.1.call-done.cot_ref.x_ref, bf16[128,2048]{1,0:T(8,128)(2,1)} %get-tuple-element.30.a_ref), custom_call_target="tpu_custom_call" | custom-call | flops 1073741824 | bytes 8388608 | tf_op jit(solution)/shard_map/pallas_call | solution.py:334
  161.1 10.7 %shard_map.106 = (f32[8,4,256,128]{3,2,1,0:T(8,128)}, bf16[2048,384]{1,0:T(8,128)(2,1)}) custom-call(s32[2]{0:T(128)} %pad_add_fusion.sibs, bf16[2048,2048]{1,0:T(8,128)(2,1)} %get-tuple-element.21.x_ref, bf16[2048,128]{1,0:T(8,128)(2,1)} %get-tuple-element.26.dq_ref, f32[2048,256]{1,0:T(8,128)} %get-tuple-element.27.own_ref, ...), custom_call_target="tpu_custom_call", output_to_operand_aliasing={{0}: (6, {})} | custom-call | flops 3221225472 | bytes 11534336 | tf_op jit(solution)/shard_map/pallas_call | solution.py:381
  171.8 4.0 %all-to-all-start.2 = ((bf16[4,512,384]{2,1,0:T(8,128)(2,1)}), bf16[4,512,384]{2,1,0:T(8,128)(2,1)S(1)}, u32[]{:S(2)}, u32[]{:S(2)}) async-start(bf16[4,512,384]{2,1,0:T(8,128)(2,1)} %bitcast.59), calls=%async_computation.2 | async-start | bytes 3145728 | tf_op jit(solution)/shard_map/all_to_all | solution.py:434
  176.5 12.2 %all-to-all-done.2.d_ref = bf16[4,512,384]{2,1,0:T(8,128)(2,1)S(1)} async-done(((bf16[4,512,384]{2,1,0:T(8,128)(2,1)}), bf16[4,512,384]{2,1,0:T(8,128)(2,1)S(1)}, u32[]{:S(2)}, u32[]{:S(2)}) %all-to-all-start.2) | async-done | bytes 1572896 | tf_op jit(solution)/shard_map/all_to_all | solution.py:434
  189.8 8.7 %shard_map.108 = (f32[4,512,128]{2,1,0:T(8,128)}, f32[4,512,128]{2,1,0:T(8,128)}, f32[4,512,128]{2,1,0:T(8,128)}, f32[4,512,128]{2,1,0:T(8,128)}) custom-call(s32[16]{0:T(128)} %stack.145.ids, bf16[4,512,384]{2,1,0:T(8,128)(2,1)} %copy-done.2, bf16[4,2048,384]{2,1,0:T(8,128)(2,1)} %bitcast.50, bf16[4,2048,384]{2,1,0:T(8,128)(2,1)} %bitcast.51, ...), custom_call_target="tpu_custom_call" | custom-call | flops 3221225472 | bytes 10485760 | tf_op jit(solution)/shard_map/pallas_call | solution.py:306
  198.5 7.0 %reduce-scatter.2.cloned.1.call-done = f32[1,4,256,128]{3,2,1,0:T(8,128)} async-done(((f32[8,4,256,128]{3,2,1,0:T(8,128)}), f32[1,4,256,128]{3,2,1,0:T(8,128)}) %reduce-scatter.2.cloned.1.call-update) | async-done | bytes 524304 | tf_op jit(solution)/shard_map/reduce_scatter | solution.py:432
  208.9 22.4 %collective-permute-done.13 = f32[4,512,128]{2,1,0:T(8,128)S(1)} collective-permute-done((f32[4,512,128]{2,1,0:T(8,128)}, f32[4,512,128]{2,1,0:T(8,128)S(1)}, u32[]{:S(2)}, u32[]{:S(2)}) %collective-permute-start.13) | collective-permute-done | bytes 1048608 | tf_op jit(solution)/shard_map/ppermute | solution.py:40
  231.3 3.6 %collective-permute-done.11 = f32[4,512,128]{2,1,0:T(8,128)S(1)} collective-permute-done((f32[4,512,128]{2,1,0:T(8,128)S(1)}, f32[4,512,128]{2,1,0:T(8,128)S(1)}, u32[]{:S(2)}, u32[]{:S(2)}) %collective-permute-start.11) | collective-permute-done | bytes 1048608 | tf_op jit(solution)/shard_map/ppermute | solution.py:40
  235.9 5.4 %all-gather.10.cloned.1.call-done = f32[32,256,128]{2,1,0:T(8,128)} async-done(((f32[4,256,128]{2,1,0:T(8,128)}), f32[32,256,128]{2,1,0:T(8,128)}) %all-gather.10.cloned.1.call-update) | async-done | bytes 4194320 | tf_op jit(solution)/shard_map/all_gather | solution.py:436
  241.2 4.1 %all-to-all-start.3 = ((bf16[4,512,128]{2,1,0:T(8,128)(2,1)}), bf16[4,512,128]{2,1,0:T(8,128)(2,1)S(1)}, u32[]{:S(2)}, u32[]{:S(2)}) async-start(bf16[4,512,128]{2,1,0:T(8,128)(2,1)} %shard_map.111), calls=%async_computation.4 | async-start | bytes 1048576 | tf_op jit(solution)/shard_map/all_to_all | solution.py:445
  245.4 3.9 %fusion = (f32[8,1,256,128]{3,2,1,0:T(8,128)S(1)}, f32[8,1,256,128]{3,2,1,0:T(8,128)}, f32[8,1,256,128]{3,2,1,0:T(8,128)}, f32[8,1,256,128]{3,2,1,0:T(8,128)}) fusion(f32[8,4,256,128]{3,2,1,0:T(8,128)} %bitcast.55), kind=kLoop, calls=%fused_computation.8 | loop fusion | bytes 8388608 | tf_op jit(solution)/shard_map/slice | solution.py:438
  (75 shorter events, 38.3 us)
Async XLA Ops:
  7.2 110.5 %all-gather.6.cloned.1.call-start = ((), (), s32[]{:S(2)}) async-start(), calls=%async_computation.5 | async-start | bytes 8912896 | tf_op jit(solution)/shard_map/all_gather | solution.py:418
  7.2 11.7 %collective-permute-start = (bf16[2048,128]{1,0:T(8,128)(2,1)}, bf16[2048,128]{1,0:T(8,128)(2,1)S(1)}, u32[]{:S(2)}, u32[]{:S(2)}) collective-permute-start(bf16[2048,128]{1,0:T(8,128)(2,1)} %param.6), channel_id=1, source_target_pairs={{0,4},{1,5},{2,6},{3,7},{4,8},{5,9},{6,10},{7,11},{8,12},{9,13},{1... | collective-permute-start | bytes 1572872 | tf_op jit(solution)/shard_map/ppermute | solution.py:40
  9.7 15.8 %collective-permute-start.2 = (bf16[2048,128]{1,0:T(8,128)(2,1)}, bf16[2048,128]{1,0:T(8,128)(2,1)S(1)}, u32[]{:S(2)}, u32[]{:S(2)}) collective-permute-start(bf16[2048,128]{1,0:T(8,128)(2,1)} %param.6), channel_id=1, source_target_pairs={{0,8},{1,9},{2,10},{3,11},{4,12},{5,13},{6,14},{7,15},{8,0},{9,1},... | collective-permute-start | bytes 1572872 | tf_op jit(solution)/shard_map/ppermute | solution.py:40
  13.0 12.5 %collective-permute-start.1 = (bf16[2048,128]{1,0:T(8,128)(2,1)}, bf16[2048,128]{1,0:T(8,128)(2,1)S(1)}, u32[]{:S(2)}, u32[]{:S(2)}) collective-permute-start(bf16[2048,128]{1,0:T(8,128)(2,1)} %param.6), channel_id=1, source_target_pairs={{0,12},{1,13},{2,14},{3,15},{4,0},{5,1},{6,2},{7,3},{8,4},{9,5},{1... | collective-permute-start | bytes 1572872 | tf_op jit(solution)/shard_map/ppermute | solution.py:40
  29.6 142.2 %all-gather.8.cloned.1.call-start = ((), (), s32[]{:S(2)}) async-start(), calls=%async_computation.7 | async-start | bytes 7864320 | tf_op jit(solution)/shard_map/all_gather | solution.py:422
  29.6 15.3 %collective-permute-start.3 = (bf16[2,2048,128]{2,1,0:T(8,128)(2,1)S(1)}, bf16[2,2048,128]{2,1,0:T(8,128)(2,1)}, u32[]{:S(2)}, u32[]{:S(2)}) collective-permute-start(bf16[2,2048,128]{2,1,0:T(8,128)(2,1)S(1)} %copy-done), channel_id=1, source_target_pairs={{0,1},{1,2},{2,3},{3,0},{4,5},{5,6},{6,7},{7,4},{8,9},{9,10},{10,1... | collective-permute-start | bytes 3145736 | tf_op jit(solution)/shard_map/ppermute | solution.py:40
  30.7 16.5 %collective-permute-start.6 = (bf16[2,2048,128]{2,1,0:T(8,128)(2,1)}, bf16[2,2048,128]{2,1,0:T(8,128)(2,1)}, u32[]{:S(2)}, u32[]{:S(2)}) collective-permute-start(bf16[2,2048,128]{2,1,0:T(8,128)(2,1)} %shard_map.102.refs_1_), channel_id=1, source_target_pairs={{0,3},{1,0},{2,1},{3,2},{4,7},{5,4},{6,5},{7,6},{8,11},{9,8},{10,9... | collective-permute-start | bytes 3145736 | tf_op jit(solution)/shard_map/ppermute | solution.py:40
  32.4 32.2 %collective-permute-start.4 = (bf16[2,2048,128]{2,1,0:T(8,128)(2,1)}, bf16[2,2048,128]{2,1,0:T(8,128)(2,1)}, u32[]{:S(2)}, u32[]{:S(2)}) collective-permute-start(bf16[2,2048,128]{2,1,0:T(8,128)(2,1)} %shard_map.102.refs_1_), channel_id=1, source_target_pairs={{0,1},{1,2},{2,3},{3,0},{4,5},{5,6},{6,7},{7,4},{8,9},{9,10},{10,1... | collective-permute-start | bytes 3145736 | tf_op jit(solution)/shard_map/ppermute | solution.py:40
  32.4 32.3 %collective-permute-start.5 = (bf16[2,2048,128]{2,1,0:T(8,128)(2,1)S(1)}, bf16[2,2048,128]{2,1,0:T(8,128)(2,1)}, u32[]{:S(2)}, u32[]{:S(2)}) collective-permute-start(bf16[2,2048,128]{2,1,0:T(8,128)(2,1)S(1)} %copy-done), channel_id=1, source_target_pairs={{0,3},{1,0},{2,1},{3,2},{4,7},{5,4},{6,5},{7,6},{8,11},{9,8},{10,9... | collective-permute-start | bytes 3145736 | tf_op jit(solution)/shard_map/ppermute | solution.py:40
  44.9 30.9 %collective-permute-start.7 = (bf16[2,2048,128]{2,1,0:T(8,128)(2,1)}, bf16[2,2048,128]{2,1,0:T(8,128)(2,1)}, u32[]{:S(2)}, u32[]{:S(2)}) collective-permute-start(bf16[2,2048,128]{2,1,0:T(8,128)(2,1)} %collective-permute-done.3.refs_2_), channel_id=1, source_target_pairs={{0,1},{1,2},{2,3},{3,0},{4,5},{5,6},{6,7},{7,4},{8,9},{9,10},{10,1... | collective-permute-start | bytes 3145736 | tf_op jit(solution)/shard_map/ppermute | solution.py:40
  47.2 32.6 %collective-permute-start.8 = (bf16[2,2048,128]{2,1,0:T(8,128)(2,1)}, bf16[2,2048,128]{2,1,0:T(8,128)(2,1)}, u32[]{:S(2)}, u32[]{:S(2)}) collective-permute-start(bf16[2,2048,128]{2,1,0:T(8,128)(2,1)} %collective-permute-done.6.refs_5_), channel_id=1, source_target_pairs={{0,3},{1,0},{2,1},{3,2},{4,7},{5,4},{6,5},{7,6},{8,11},{9,8},{10,9... | collective-permute-start | bytes 3145736 | tf_op jit(solution)/shard_map/ppermute | solution.py:40
  53.4 26.5 %copy-start.1 = (bf16[2048,384]{1,0:T(8,128)(2,1)}, bf16[2048,384]{1,0:T(8,128)(2,1)S(1)}, u32[]{:S(2)}) copy-start(bf16[2048,384]{1,0:T(8,128)(2,1)S(1)} %constant_dynamic-update-slice_fusion.refs_8_.x_ref) | copy-start | bytes 4718596
  92.9 17.5 %all-to-all-start = ((bf16[8,64,256]{2,1,0:T(8,128)(2,1)}), bf16[8,64,256]{2,1,0:T(8,128)(2,1)S(1)}, u32[]{:S(2)}, u32[]{:S(2)}) async-start(bf16[8,64,256]{2,1,0:T(8,128)(2,1)} %get-tuple-element.25), calls=%async_computation | async-start | bytes 524288 | tf_op jit(solution)/shard_map/all_to_all | solution.py:420
  103.9 1.3 collective-permute-start.9
  145.3 14.9 %all-to-all-start.1 = ((f32[8,64,256]{2,1,0:T(8,128)}), f32[8,64,256]{2,1,0:T(8,128)S(1)}, u32[]{:S(2)}, u32[]{:S(2)}) async-start(f32[8,64,256]{2,1,0:T(8,128)} %get-tuple-element.29), calls=%async_computation.1 | async-start | bytes 1048576 | tf_op jit(solution)/shard_map/all_to_all | solution.py:429
  150.8 54.8 %reduce-scatter.2.cloned.1.call-start = ((), (), s32[]{:S(2)}) async-start(), calls=%async_computation.6 | async-start | bytes 4718592 | tf_op jit(solution)/shard_map/reduce_scatter | solution.py:432
  150.8 6.3 %collective-permute-start.10 = (f32[128,256]{1,0:T(8,128)}, f32[128,256]{1,0:T(8,128)S(1)}, u32[]{:S(2)}, u32[]{:S(2)}) collective-permute-start(f32[128,256]{1,0:T(8,128)} %get-tuple-element.28), channel_id=1, source_target_pairs={{0,16},{16,0},{32,48},{48,32},{64,80},{80,64},{96,112},{112,96},{1... | collective-permute-start | bytes 393224 | tf_op jit(solution)/shard_map/ppermute | solution.py:57
  171.8 16.9 %all-to-all-start.2 = ((bf16[4,512,384]{2,1,0:T(8,128)(2,1)}), bf16[4,512,384]{2,1,0:T(8,128)(2,1)S(1)}, u32[]{:S(2)}, u32[]{:S(2)}) async-start(bf16[4,512,384]{2,1,0:T(8,128)(2,1)} %bitcast.59), calls=%async_computation.2 | async-start | bytes 3145728 | tf_op jit(solution)/shard_map/all_to_all | solution.py:434
  175.8 65.5 %all-gather.10.cloned.1.call-start = ((), (), s32[]{:S(2)}) async-start(), calls=%async_computation.8 | async-start | bytes 4718592 | tf_op jit(solution)/shard_map/all_gather | solution.py:436
  198.5 36.3 %copy-start.3 = (f32[4,512,128]{2,1,0:T(8,128)S(1)}, f32[4,512,128]{2,1,0:T(8,128)}, u32[]{:S(2)}) copy-start(f32[4,512,128]{2,1,0:T(8,128)} %get-tuple-element.32.dep_ref) | copy-start | bytes 3145732
  205.6 25.7 %collective-permute-start.13 = (f32[4,512,128]{2,1,0:T(8,128)}, f32[4,512,128]{2,1,0:T(8,128)S(1)}, u32[]{:S(2)}, u32[]{:S(2)}) collective-permute-start(f32[4,512,128]{2,1,0:T(8,128)} %get-tuple-element.35), channel_id=1, source_target_pairs={{0,3},{1,0},{2,1},{3,2},{4,7},{5,4},{6,5},{7,6},{8,11},{9,8},{10,9... | collective-permute-start | bytes 3145736 | tf_op jit(solution)/shard_map/ppermute | solution.py:40
  207.9 23.3 %collective-permute-start.12 = (f32[4,512,128]{2,1,0:T(8,128)}, f32[4,512,128]{2,1,0:T(8,128)S(1)}, u32[]{:S(2)}, u32[]{:S(2)}) collective-permute-start(f32[4,512,128]{2,1,0:T(8,128)} %get-tuple-element.34), channel_id=1, source_target_pairs={{0,2},{1,3},{2,0},{3,1},{4,6},{5,7},{6,4},{7,5},{8,10},{9,11},{10,... | collective-permute-start | bytes 3145736 | tf_op jit(solution)/shard_map/ppermute | solution.py:40
  208.3 26.5 %collective-permute-start.11 = (f32[4,512,128]{2,1,0:T(8,128)S(1)}, f32[4,512,128]{2,1,0:T(8,128)S(1)}, u32[]{:S(2)}, u32[]{:S(2)}) collective-permute-start(f32[4,512,128]{2,1,0:T(8,128)S(1)} %copy-done.10), channel_id=1, source_target_pairs={{0,1},{1,2},{2,3},{3,0},{4,5},{5,6},{6,7},{7,4},{8,9},{9,10},{10,1... | collective-permute-start | bytes 3145736 | tf_op jit(solution)/shard_map/ppermute | solution.py:40
  241.2 11.4 %all-to-all-start.3 = ((bf16[4,512,128]{2,1,0:T(8,128)(2,1)}), bf16[4,512,128]{2,1,0:T(8,128)(2,1)S(1)}, u32[]{:S(2)}, u32[]{:S(2)}) async-start(bf16[4,512,128]{2,1,0:T(8,128)(2,1)} %shard_map.111), calls=%async_computation.4 | async-start | bytes 1048576 | tf_op jit(solution)/shard_map/all_to_all | solution.py:445
  (11 other events, 101.3 us)
Sparse Core Ops, SparseCore 0:
  29.7 87.9 all-gather.5
  119.3 41.4 all-gather.7
  171.9 33.5 reduce-scatter.1
  207.1 34.0 all-gather.9
